TPU v7x, 512 devices: a whole 4x4x16 slice. The times are simulated.
512 devices in a mesh: dp: 8 (over z_lo), row: 8 (over x, core), col: 8 (over z_hi, y).
Axes of the slice: x: 4, y: 4, z: 16 (z_hi: 2, z_lo: 8; z = z_hi * 8 + z_lo), core: 2. Of those that a mesh axis runs over, the one named last changes fastest.
Arguments:
- patches: bfloat16 [512, 6144], P(('dp', 'row'), 'col'), may hold values from -6 to 6
- w_up: bfloat16 [6144, 24576], P('col', ('dp', 'row')), may hold values from -0.078125 to 0.078125
- w_down: bfloat16 [24576, 6144], P(('dp', 'row'), 'col'), may hold values from -0.0390625 to 0.0390625
- owner_route: int32 [512], P(('dp', 'row')), may hold values from 0 to 7, as said below
- tok_grad: bfloat16 [512, 6144], P(('dp', 'row'), 'col'), may hold values from -0.1875 to 0.1875
- pool_grad: bfloat16 [64, 6144], P(('dp', 'row'), 'col'), may hold values from -1.5 to 1.5
Outputs:
- mixed: bfloat16 [512, 6144], P(('dp', 'row'), 'col')
- pooled: float32 [64, 6144], P(('dp', 'row'), 'col')
- grad_up: float32 [6144, 24576], P('col', ('dp', 'row'))
- grad_down: float32 [24576, 6144], P(('dp', 'row'), 'col')
Inputs may be any that keep to these rules, and one draw needn't show every extreme that they name: `owner_route`: each device of dp and row holds 8 tokens, of which at most 2 name any one owner; in every dp group some owner is named exactly 2 times by every device of that group, and some other owner by no device of that group.
All inputs are finite; a program needn't handle non-finite values.
Results may differ from a plain program's by a relative error of at most 0.0054.
Values may be sent and summed in bfloat16 or wider, within the bound.
No kernel may reach another device: no remote copies, remote signals or barrier semaphores. Data moves between devices by JAX's collectives and lax.ppermute only.
A program may use at most 64 MiB of HBM per device.

v0:
```python
import math

import jax
import jax.numpy as jnp
from jax import lax
from jax.sharding import PartitionSpec as P

GELU_SCALE = math.sqrt(2.0 / math.pi)


def gelu_tanh(inner):
    return 0.5 * inner * (1.0 + jnp.tanh(GELU_SCALE * (inner + 0.044715 * inner * inner * inner)))


def gelu_slope(inner):
    tanh_term = jnp.tanh(GELU_SCALE * (inner + 0.044715 * inner * inner * inner))
    return 0.5 * (1.0 + tanh_term) + 0.5 * inner * (1.0 - tanh_term * tanh_term) * GELU_SCALE * (
        1.0 + 3.0 * 0.044715 * inner * inner
    )


def token_rows(shard_rows):
    return lax.all_gather(shard_rows, ("dp", "row"), axis=0, tiled=True)


def col_total(partial_term):
    return lax.psum(partial_term, "col")


def local(patches, w_up, w_down, owner_route, tok_grad, pool_grad):
    tok_dev = patches.shape[0]
    row_count = lax.axis_size("row")
    slot_cap = max(2, (tok_dev + row_count - 2) // (row_count - 1))
    all_rows = token_rows(patches)
    up_term = jnp.dot(all_rows, w_up, preferred_element_type=jnp.float32)
    preact_part = col_total(up_term)
    hidden = gelu_tanh(preact_part).astype(jnp.bfloat16)
    summed = lax.psum_scatter(
        jnp.dot(hidden, w_down, preferred_element_type=jnp.float32),
        ("dp", "row"),
        scatter_dimension=0,
        tiled=True,
    )
    mixed_rows = summed.astype(jnp.bfloat16)
    owner_ids = lax.broadcasted_iota(jnp.int32, (row_count, tok_dev), 0)
    to_owner = (owner_route[None, :] == owner_ids).astype(jnp.float32)
    earlier = jnp.cumsum(to_owner, axis=1) - to_owner
    slot_of = jnp.sum(earlier * to_owner, axis=0)
    slot_ids = lax.broadcasted_iota(jnp.float32, (1, slot_cap, 1), 1)
    placing = to_owner[:, None, :] * (slot_of[None, None, :] == slot_ids).astype(jnp.float32)
    placing_bf = placing.astype(jnp.bfloat16)
    outgoing = jnp.einsum(
        "ost,td->osd", placing_bf, mixed_rows, preferred_element_type=jnp.float32
    ).astype(jnp.bfloat16)
    filled = jnp.sum(placing, axis=2).astype(jnp.bfloat16)
    arrived, present = (
        lax.all_to_all(outgoing, "row", split_axis=0, concat_axis=0, tiled=True),
        lax.all_to_all(filled, "row", split_axis=0, concat_axis=0, tiled=True),
    )
    total_sum = jnp.sum(arrived.astype(jnp.float32), axis=(0, 1))[None, :]
    count_sum = jnp.sum(present.astype(jnp.float32)).reshape(1)
    divisor = jnp.maximum(count_sum, 1.0)
    pooled = total_sum / divisor[:, None]
    image_grad = (pool_grad.astype(jnp.float32) / divisor[:, None]).astype(jnp.bfloat16)
    grad_slots = present[:, :, None] * image_grad[None, :, :]
    came_back = lax.all_to_all(grad_slots, "row", split_axis=0, concat_axis=0, tiled=True)
    returned = jnp.einsum("ost,osd->td", placing_bf, came_back, preferred_element_type=jnp.float32)
    grad_mixed = (tok_grad.astype(jnp.float32) + returned).astype(jnp.bfloat16)
    all_grads = token_rows(grad_mixed)
    back_term = lax.dot_general(
        all_grads, w_down, (((1,), (1,)), ((), ())), preferred_element_type=jnp.float32
    )
    grad_preact = (col_total(back_term) * gelu_slope(preact_part)).astype(jnp.bfloat16)
    grad_down = lax.dot_general(
        hidden, all_grads, (((0,), (0,)), ((), ())), preferred_element_type=jnp.float32
    )
    grad_up = lax.dot_general(
        all_rows, grad_preact, (((0,), (0,)), ((), ())), preferred_element_type=jnp.float32
    )
    return (mixed_rows, pooled, grad_up, grad_down)


def solution(mesh):
    in_specs = (
        P(("dp", "row"), "col"),
        P("col", ("dp", "row")),
        P(("dp", "row"), "col"),
        P(("dp", "row")),
        P(("dp", "row"), "col"),
        P(("dp", "row"), "col"),
    )
    out_specs = (
        P(("dp", "row"), "col"),
        P(("dp", "row"), "col"),
        P("col", ("dp", "row")),
        P(("dp", "row"), "col"),
    )
    return jax.shard_map(local, mesh=mesh, in_specs=in_specs, out_specs=out_specs, check_vma=False)
```

profile of v0, /device:TPU:1, one launch (start us, length us, event | category | flops | bytes accessed | tf_op | source)
XLA Modules:
  0.0 923.6 jit_solution(15033958824273122560)
XLA Ops:
  7.2 0.8 fusion.21
  8.0 0.8 select_reduce_fusion
  8.9 0.1 multiply_reduce_fusion
  9.0 0.7 copy.14
  9.7 10.1 %all-to-all-start.1 = ((bf16[8,1,2]{2,1,0:T(2,128)(2,1)}), bf16[8,1,2]{2,1,0:T(2,128)(2,1)S(1)}, u32[]{:S(2)}, u32[]{:S(2)}) async-start(bf16[8,1,2]{2,1,0:T(2,128)(2,1)} %copy.14), calls=%async_computation.2 | async-start | bytes 8192 | tf_op jit(solution)/shard_map/all_to_all | solution.py:58
  19.8 123.9 %all_gather.6 = bf16[512,768]{1,0:T(8,128)(2,1)S(1)} all-gather(bf16[8,768]{1,0:T(8,128)(2,1)} %param.6), channel_id=1, replica_groups=mesh['dp'=8,'row'=8,'col'=8] {'dp','row'}, dimensions={0}, use_global_device_ids=true | all-gather | bytes 798720 | tf_op jit(solution)/shard_map/all_gather | solution.py:23
  143.6 0.1 copy.15
  143.7 0.6 convert_reduce_fusion.2
  144.3 0.1 copy.16
  145.1 0.7 convert_reduce_fusion.1
  145.8 0.7 broadcast_multiply_fusion
  146.5 3.4 all-to-all-start.2
  149.9 1.5 fusion.29
  151.4 3.2 all-to-all-done.2
  154.6 0.3 fusion.1
  154.9 115.3 %all_gather.7 = bf16[512,768]{1,0:T(8,128)(2,1)S(1)} all-gather(bf16[8,768]{1,0:T(8,128)(2,1)S(1)} %fusion.1), channel_id=1, replica_groups=mesh['dp'=8,'row'=8,'col'=8] {'dp','row'}, dimensions={0}, use_global_device_ids=true | all-gather | bytes 798720 | tf_op jit(solution)/shard_map/all_gather | solution.py:23
  270.1 1.5 fusion.30
  271.6 0.0 all-reduce.3.cloned.1.call-update
  271.6 0.0 reduce-scatter.2.cloned.1.call-start
  271.7 193.0 %all-reduce.3.cloned.1.call-done = (f32[512,384]{1,0:T(8,128)}, f32[512,384]{1,0:T(8,128)}) async-done(((f32[512,384]{1,0:T(8,128)}, f32[512,384]{1,0:T(8,128)}), (f32[512,384]{1,0:T(8,128)}, f32[512,384]{1,0:T(8,128)})) %all-reduce.3.cloned.1.call-update) | async-done | bytes 1572880 | tf_op jit(solution)/shard_map/psum | solution.py:27
  464.6 3.0 fusion.28
  467.6 0.0 reduce-scatter.2.cloned.1.call-update
  467.6 2.2 convolution_bitcast_fusion
  469.8 426.4 %reduce-scatter.2.cloned.1.call-done = f32[8,768]{1,0:T(8,128)} async-done(((f32[512,768]{1,0:T(8,128)}), f32[8,768]{1,0:T(8,128)}) %reduce-scatter.2.cloned.1.call-update) | async-done | bytes 24592 | tf_op jit(solution)/shard_map/reduce_scatter | solution.py:38
  896.3 0.7 convert_element_type.62
  897.0 0.3 convolution_convert_fusion
  897.3 0.6 copy.13
  897.9 13.6 %all-to-all-start = ((bf16[8,2,768]{2,1,0:T(2,128)(2,1)}), bf16[8,2,768]{2,1,0:T(2,128)(2,1)S(1)}, u32[]{:S(2)}, u32[]{:S(2)}) async-start(bf16[8,2,768]{2,1,0:T(2,128)(2,1)} %copy.13), calls=%async_computation.1 | async-start | bytes 49152 | tf_op jit(solution)/shard_map/all_to_all | solution.py:57
  911.5 2.7 fusion.27
  914.2 1.4 copy.18
  915.6 0.6 all-to-all-done
  916.2 0.6 div.29
  (14 shorter events, 0.1 us)
Async XLA Ops:
  7.2 263.0 %copy-start = (bf16[384,768]{1,0:T(8,128)(2,1)S(1)}, bf16[384,768]{1,0:T(8,128)(2,1)}, u32[]{:S(2)}) copy-start(bf16[384,768]{1,0:T(8,128)(2,1)} %param.8) | copy-start | bytes 1769476
  7.2 142.7 %copy-start.1 = (bf16[768,384]{1,0:T(8,128)(2,1)S(1)}, bf16[768,384]{1,0:T(8,128)(2,1)}, u32[]{:S(2)}) copy-start(bf16[768,384]{1,0:T(8,128)(2,1)} %param.7) | copy-start | bytes 1769476
  9.7 134.0 %all-to-all-start.1 = ((bf16[8,1,2]{2,1,0:T(2,128)(2,1)}), bf16[8,1,2]{2,1,0:T(2,128)(2,1)S(1)}, u32[]{:S(2)}, u32[]{:S(2)}) async-start(bf16[8,1,2]{2,1,0:T(2,128)(2,1)} %copy.14), calls=%async_computation.2 | async-start | bytes 8192 | tf_op jit(solution)/shard_map/all_to_all | solution.py:58
  143.6 11.0 %copy-start.3 = (bf16[8,768]{1,0:T(8,128)(2,1)S(1)}, bf16[8,768]{1,0:T(8,128)(2,1)}, u32[]{:S(2)}) copy-start(bf16[8,768]{1,0:T(8,128)(2,1)} %param.10) | copy-start | bytes 36868
  146.5 8.1 all-to-all-start.2
  149.9 314.8 %all-reduce.3.cloned.1.call-start = ((), (), s32[]{:S(2)}) async-start(), calls=%async_computation.5 | async-start | bytes 3145728 | tf_op jit(solution)/shard_map/psum | solution.py:27
  271.6 624.6 %reduce-scatter.2.cloned.1.call-start = ((), (), s32[]{:S(2)}) async-start(), calls=%async_computation.4 | async-start | bytes 1597440 | tf_op jit(solution)/shard_map/reduce_scatter | solution.py:38
  897.0 17.2 %copy-start.2 = (bf16[8,768]{1,0:T(8,128)(2,1)}, bf16[8,768]{1,0:T(8,128)(2,1)S(1)}, u32[]{:S(2)}) copy-start(bf16[8,768]{1,0:T(8,128)(2,1)S(1)} %convert_element_type.62) | copy-start | bytes 36868
  897.9 18.3 %all-to-all-start = ((bf16[8,2,768]{2,1,0:T(2,128)(2,1)}), bf16[8,2,768]{2,1,0:T(2,128)(2,1)S(1)}, u32[]{:S(2)}, u32[]{:S(2)}) async-start(bf16[8,2,768]{2,1,0:T(2,128)(2,1)} %copy.13), calls=%async_computation.1 | async-start | bytes 49152 | tf_op jit(solution)/shard_map/all_to_all | solution.py:57
Sparse Core Ops, SparseCore 0:
  271.8 192.8 all-reduce.2
  467.7 428.4 reduce-scatter.1
where the time goes:
time: 924 us
  waiting for transfers between devices  623 us (67%)
  blocking collectives  239 us (26%)
  starting transfers between devices  27.1 us (3%)
  between operations  14.7 us (2%)
  matrix products  11.4 us (1%)
    reduce_scatter x1, waiting for transfers between devices, local(): lax.psum_scatter(jnp.dot(hidden, w_down, preferred_element_type=jnp.float...  426 us
    all_gather x2, blocking collectives, token_rows(): return lax.all_gather(shard_rows, ('dp', 'row'), axis=0, tiled=True)  239 us
    psum x1, waiting for transfers between devices, col_total(): return lax.psum(partial_term, 'col')  193 us
  transfers between devices with their start and end apart: 5, of which 4 were waited for; matrix products, arithmetic and copies ran while one was open for 1% of the time, Pallas kernels for 0%

commit v1 on v0

v1 whole, which is shorter than its diff:
```python
import math

import jax
import jax.numpy as jnp
from jax import lax
from jax.sharding import PartitionSpec as P

GELU_SCALE = math.sqrt(2.0 / math.pi)
BF = jnp.bfloat16
F32 = jnp.float32
LANES = 128

Y_GROUPS = [[0, 1, 2, 3], [4, 5, 6, 7]]
X_GROUPS = [[0, 2, 4, 6], [1, 3, 5, 7]]
CORE_GROUPS = [[0, 1], [2, 3], [4, 5], [6, 7]]
Z_SWAP = [(i, (i + 4) % 8) for i in range(8)]


def spread(block, axis, count, groups=None):
    copies = jnp.broadcast_to(block[None], (count,) + block.shape)
    return lax.all_to_all(copies, axis, split_axis=0, concat_axis=0, tiled=True, axis_index_groups=groups)


def exchange(blocks, axis, groups=None):
    return lax.all_to_all(blocks, axis, split_axis=0, concat_axis=0, tiled=True, axis_index_groups=groups)


def local(patches, w_up, w_down, owner_route, tok_grad, pool_grad):
    tok, width = patches.shape
    hid = w_up.shape[1]
    pieces = width // LANES

    side = jnp.concatenate(
        [
            pool_grad.reshape(pieces, LANES),
            jnp.pad(owner_route.astype(BF)[None, :], ((0, 0), (0, LANES - tok))),
            jnp.zeros((tok - pieces - 1, LANES), BF),
        ],
        axis=0,
    )
    block = jnp.concatenate([patches, tok_grad, side], axis=1)
    got = spread(block, "dp", 8)
    got = got.reshape(64, 2 * width + LANES)
    got = spread(got, "row", 4, X_GROUPS)
    got = got.reshape(256, 2 * width + LANES)
    got = spread(got, "row", 2, CORE_GROUPS)
    got = got.reshape(512, 2 * width + LANES)

    rows = got[:, :width]
    tgrads = got[:, width : 2 * width]
    sides = got[:, 2 * width :].reshape(64, tok, LANES)
    pools = sides[:, :pieces, :].reshape(64, width)
    route = sides[:, pieces, :tok].astype(jnp.int32)
    dp_of = lax.broadcasted_iota(jnp.int32, (64, tok), 0) % 8
    image = ((route % 2) * 4 + route // 2) * 8 + dp_of
    image = image.reshape(512, 1)
    onehot = (image == lax.broadcasted_iota(jnp.int32, (512, 64), 1)).astype(BF)
    count = jnp.maximum(jnp.sum(onehot.astype(F32), axis=0), 1.0)[:, None]
    image_grad = (pools.astype(F32) / count).astype(BF)
    returned = jnp.dot(onehot, image_grad, preferred_element_type=F32)
    grads = (tgrads.astype(F32) + returned).astype(BF)

    up = jnp.dot(rows, w_up, preferred_element_type=F32)
    back = lax.dot_general(grads, w_down, (((1,), (1,)), ((), ())), preferred_element_type=F32)
    both = jnp.concatenate([up.astype(BF), back.astype(BF)], axis=1).reshape(4, 128, 2 * hid)
    part = exchange(both, "col", Y_GROUPS)
    part = jnp.sum(part.astype(F32), axis=0).astype(BF)
    other = lax.ppermute(part, "col", Z_SWAP)
    total = part.astype(F32) + other.astype(F32)
    v = total[:, :hid]
    s = jnp.tanh(GELU_SCALE * (v + 0.044715 * v * v * v))
    hidden = (0.5 * v * (1.0 + s)).astype(BF)
    slope = 0.5 * (1.0 + s) + 0.5 * v * (1.0 - s * s) * GELU_SCALE * (1.0 + 3.0 * 0.044715 * v * v)
    gp = (total[:, hid:] * slope).astype(BF)
    hg = spread(jnp.concatenate([hidden, gp], axis=1), "col", 4, Y_GROUPS).reshape(512, 2 * hid)
    hidden = hg[:, :hid]
    gp = hg[:, hid:]

    down = jnp.dot(hidden, w_down, preferred_element_type=F32)
    pooled_part = (
        lax.dot_general(onehot, down.astype(BF), (((0,), (0,)), ((), ())), preferred_element_type=F32) / count
    )
    packed = jnp.pad(pooled_part.astype(BF).reshape(64, pieces, LANES), ((0, 0), (0, tok - pieces), (0, 0)))
    down = jnp.concatenate([down.astype(BF), packed.reshape(512, LANES)], axis=1)
    down = down.reshape(2, 4, 64, width + LANES).transpose(1, 0, 2, 3).reshape(8, 64, width + LANES)
    half = exchange(down, "row")
    half = jnp.sum(half.astype(F32), axis=0).astype(BF).reshape(8, tok, width + LANES)
    last = exchange(half, "dp")
    last = jnp.sum(last.astype(F32), axis=0)
    mixed = last[:, :width].astype(BF)
    pooled = last[:pieces, width:].reshape(1, width)

    grad_down = lax.dot_general(hidden, grads, (((0,), (0,)), ((), ())), preferred_element_type=F32)
    grad_up = lax.dot_general(rows, gp, (((0,), (0,)), ((), ())), preferred_element_type=F32)
    return (mixed, pooled, grad_up, grad_down)


def solution(mesh):
    in_specs = (
        P(("dp", "row"), "col"),
        P("col", ("dp", "row")),
        P(("dp", "row"), "col"),
        P(("dp", "row")),
        P(("dp", "row"), "col"),
        P(("dp", "row"), "col"),
    )
    out_specs = (
        P(("dp", "row"), "col"),
        P(("dp", "row"), "col"),
        P("col", ("dp", "row")),
        P(("dp", "row"), "col"),
    )
    return jax.shard_map(local, mesh=mesh, in_specs=in_specs, out_specs=out_specs, check_vma=False)
```

time: 924 us -> 153 us (0.17)
  waiting for transfers between devices: 623 us -> 21.8 us
  blocking collectives: 239 us -> 83.3 us
  between operations: 14.7 us -> 0.85 us
    reduce_scatter x1 -> x0, waiting for transfers between devices: 426 us -> none  [local(): lax.psum_scatter(jnp.dot(hidden, w_down, preferred_element_type=jnp.float...]
    all_gather x2 -> x0, blocking collectives: 239 us -> none  [token_rows(): return lax.all_gather(shard_rows, ('dp', 'row'), axis=0, tiled=True)]
    psum x1 -> x0, waiting for transfers between devices: 193 us -> none  [col_total(): return lax.psum(partial_term, 'col')]
    all_to_all x0 -> x5, blocking collectives: none -> 83.3 us  [the longest x3 45.2 us: spread(): lax.all_to_all(copies, axis, split_axis=0, concat_axis=0, tiled=True, axi...]
    all_to_all x3 -> x2, waiting for transfers between devices: 3.82 us -> 14.4 us  [the longest x1 8.51 us: spread(): lax.all_to_all(copies, axis, split_axis=0, concat_axis=0, tiled=True, axi...]
    all_to_all x3 -> x2, starting transfers between devices: 27.1 us -> 24.7 us  [the longest x1 20.7 us: exchange(): lax.all_to_all(blocks, axis, split_axis=0, concat_axis=0, tiled=True, axi...]
  transfers between devices with their start and end apart: 5 -> 3, of which waited for: 4 -> 3; matrix products, arithmetic and copies ran while one was open for 1% -> 3% of each run, Pallas kernels for 0% -> 0%
where the time goes in v1:
time: 153 us; the launch traced here: 152 us
  blocking collectives  83.3 us (54%)
  starting transfers between devices  32.7 us (21%)
  waiting for transfers between devices  21.8 us (14%)
  matrix products  6.52 us (4%)
  other arithmetic  3.97 us (3%)
  local copies, waits for them, and re-layouts  2.94 us (2%)
    all_to_all x3, blocking collectives, spread(): lax.all_to_all(copies, axis, split_axis=0, concat_axis=0, tiled=True, axi...  45.2 us
    all_to_all x2, blocking collectives, exchange(): lax.all_to_all(blocks, axis, split_axis=0, concat_axis=0, tiled=True, axi...  38.1 us
    all_to_all x1, starting transfers between devices, exchange(): lax.all_to_all(blocks, axis, split_axis=0, concat_axis=0, tiled=True, axi...  20.7 us
    all_to_all x1, waiting for transfers between devices, spread(): lax.all_to_all(copies, axis, split_axis=0, concat_axis=0, tiled=True, axi...  8.51 us
    ppermute x1, starting transfers between devices, local(): other = lax.ppermute(part, 'col', Z_SWAP)  7.95 us
    ppermute x1, waiting for transfers between devices, local(): other = lax.ppermute(part, 'col', Z_SWAP)  7.42 us
    all_to_all x1, waiting for transfers between devices, exchange(): lax.all_to_all(blocks, axis, split_axis=0, concat_axis=0, tiled=True, axi...  5.91 us
    all_to_all x1, starting transfers between devices, spread(): lax.all_to_all(copies, axis, split_axis=0, concat_axis=0, tiled=True, axi...  4.01 us
  transfers between devices with their start and end apart: 3, of which 3 were waited for; matrix products, arithmetic and copies ran while one was open for 3% of the time, Pallas kernels for 0%

profile of v1, /device:TPU:1, one launch (start us, length us, event | category | flops | bytes accessed | tf_op | source)
XLA Modules:
  0.0 152.1 jit_solution(1850202359631316546)
XLA Ops:
  0.6 0.7 convert_bitcast_fusion
  1.4 0.7 reduce.2
  2.1 0.7 fusion.28
  2.8 24.2 %all_to_all.35 = bf16[8,8,1664]{2,1,0:T(8,128)(2,1)S(1)} all-to-all(bf16[8,8,1664]{2,1,0:T(8,128)(2,1)S(1)} %broadcast_in_dim.35), channel_id=1, replica_groups=mesh['dp'=8,'row'=8,'col'=8] {'dp'}, dimensions={0} | all-to-all | bytes 425984 | tf_op jit(solution)/shard_map/all_to_all | solution.py:21
  27.1 1.0 broadcast_in_dim.37
  28.0 4.0 %all-to-all-start.1 = ((bf16[4,64,1664]{2,1,0:T(8,128)(2,1)}), bf16[4,64,1664]{2,1,0:T(8,128)(2,1)S(1)}, u32[]{:S(2)}, u32[]{:S(2)}) async-start(bf16[4,64,1664]{2,1,0:T(8,128)(2,1)} %broadcast_in_dim.37), calls=%async_computation.1 | async-start | bytes 1703936 | tf_op jit(solution)/shard_map/all_to_all | solution.py:21
  32.2 8.5 %all-to-all-done.1 = bf16[4,64,1664]{2,1,0:T(8,128)(2,1)S(1)} async-done(((bf16[4,64,1664]{2,1,0:T(8,128)(2,1)}), bf16[4,64,1664]{2,1,0:T(8,128)(2,1)S(1)}, u32[]{:S(2)}, u32[]{:S(2)}) %all-to-all-start.1) | async-done | bytes 852000 | tf_op jit(solution)/shard_map/all_to_all | solution.py:21
  40.7 0.1 broadcast_in_dim.39
  40.9 10.3 %all_to_all.36 = bf16[2,256,1664]{2,1,0:T(8,128)(2,1)S(1)} all-to-all(bf16[2,256,1664]{2,1,0:T(8,128)(2,1)S(1)} %broadcast_in_dim.39), channel_id=1, replica_groups={{0,8},{16,24},{32,40},{48,56},{1,9},{17,25},{33,41},{49,57},{2,10},{18,..., dimensions={0} | all-to-all | bytes 3407872 | tf_op jit(solution)/shard_map/all_to_all | solution.py:21
  51.2 0.1 fusion.25
  51.6 0.5 convolution_convert_fusion.2
  52.1 0.4 add_convert_fusion
  52.6 0.5 convolution_convert_fusion.1
  53.1 0.1 copy_bitcast_fusion
  53.2 15.4 %all_to_all.37 = bf16[4,128,768]{1,2,0:T(8,128)(2,1)S(1)} all-to-all(bf16[4,128,768]{1,2,0:T(8,128)(2,1)S(1)} %copy_bitcast_fusion), channel_id=1, replica_groups={{0,1,2,3},{4,5,6,7},{8,9,10,11},{12,13,14,15},{16,17,18,19},{20,21,22,2..., dimensions={0} | all-to-all | bytes 1572864 | tf_op jit(solution)/shard_map/all_to_all | solution.py:25
  68.6 0.2 reduce_sum.43
  68.8 7.9 %collective-permute-start = (bf16[128,768]{0,1:T(8,128)(2,1)S(1)}, bf16[128,768]{0,1:T(8,128)(2,1)S(1)}, u32[]{:S(2)}, u32[]{:S(2)}) collective-permute-start(bf16[128,768]{0,1:T(8,128)(2,1)S(1)} %reduce_sum.43), channel_id=1, source_target_pairs={{0,4},{1,5},{2,6},{3,7},{4,0},{5,1},{6,2},{7,3},{8,12},{9,13},{10,... | collective-permute-start | bytes 589832 | tf_op jit(solution)/shard_map/ppermute | solution.py:68
  76.7 7.4 %collective-permute-done = bf16[128,768]{0,1:T(8,128)(2,1)S(1)} collective-permute-done((bf16[128,768]{0,1:T(8,128)(2,1)S(1)}, bf16[128,768]{0,1:T(8,128)(2,1)S(1)}, u32[]{:S(2)}, u32[]{:S(2)}) %collective-permute-start) | collective-permute-done | bytes 196640 | tf_op jit(solution)/shard_map/ppermute | solution.py:68
  84.2 0.1 multiply_convert_fusion
  84.4 0.1 copy.19
  84.6 10.7 %all_to_all.38 = bf16[4,128,768]{2,1,0:T(8,128)(2,1)S(1)} all-to-all(bf16[4,128,768]{2,1,0:T(8,128)(2,1)S(1)} %broadcast_in_dim.40), channel_id=1, replica_groups={{0,1,2,3},{4,5,6,7},{8,9,10,11},{12,13,14,15},{16,17,18,19},{20,21,22,2..., dimensions={0} | all-to-all | bytes 1572864 | tf_op jit(solution)/shard_map/all_to_all | solution.py:21
  95.3 0.6 convolution_convert_fusion
  95.9 0.2 fusion
  96.1 0.1 reshape.121
  96.5 22.7 %all_to_all.39 = bf16[8,64,896]{2,1,0:T(8,128)(2,1)S(1)} all-to-all(bf16[8,64,896]{2,1,0:T(8,128)(2,1)S(1)} %bitcast.38), channel_id=1, replica_groups=mesh['dp'=8,'row'=8,'col'=8] {'row'}, dimensions={0} | all-to-all | bytes 1835008 | tf_op jit(solution)/shard_map/all_to_all | solution.py:25
  119.2 0.8 reduce_sum.44
  120.0 20.7 %all-to-all-start.6 = ((bf16[8,8,896]{2,1,0:T(8,128)(2,1)}), bf16[8,8,896]{2,1,0:T(8,128)(2,1)S(1)}, u32[]{:S(2)}, u32[]{:S(2)}) async-start(bf16[8,8,896]{2,1,0:T(8,128)(2,1)} %bitcast.10), calls=%async_computation.6 | async-start | bytes 229376 | tf_op jit(solution)/shard_map/all_to_all | solution.py:25
  140.7 2.7 %fusion.1 = f32[768,384]{1,0:T(8,128)} fusion(bf16[512,1664]{1,0:T(8,128)(2,1)} %bitcast.47, bf16[512,768]{1,0:T(8,128)(2,1)S(1)} %bitcast.42), kind=kOutput, calls=%fused_computation.9 | convolution fusion | flops 301989888 | bytes 2359296 | tf_op jit(solution)/shard_map/dot_general | solution.py:94
  143.4 1.5 fusion.5
  145.0 5.9 %all-to-all-done.6 = bf16[8,8,896]{2,1,0:T(8,128)(2,1)S(1)} async-done(((bf16[8,8,896]{2,1,0:T(8,128)(2,1)}), bf16[8,8,896]{2,1,0:T(8,128)(2,1)S(1)}, u32[]{:S(2)}, u32[]{:S(2)}) %all-to-all-start.6) | async-done | bytes 114720 | tf_op jit(solution)/shard_map/all_to_all | solution.py:25
  150.9 0.6 slice.82
  151.5 0.6 copy.31
  (26 shorter events, 0.8 us)
Async XLA Ops:
  0.6 51.9 %copy-start = (bf16[384,768]{1,0:T(8,128)(2,1)S(1)}, bf16[384,768]{1,0:T(8,128)(2,1)}, u32[]{:S(2)}) copy-start(bf16[384,768]{1,0:T(8,128)(2,1)} %param.8) | copy-start | bytes 1769476
  28.0 12.7 %all-to-all-start.1 = ((bf16[4,64,1664]{2,1,0:T(8,128)(2,1)}), bf16[4,64,1664]{2,1,0:T(8,128)(2,1)S(1)}, u32[]{:S(2)}, u32[]{:S(2)}) async-start(bf16[4,64,1664]{2,1,0:T(8,128)(2,1)} %broadcast_in_dim.37), calls=%async_computation.1 | async-start | bytes 1703936 | tf_op jit(solution)/shard_map/all_to_all | solution.py:21
  40.9 10.7 %copy-start.2 = (bf16[768,384]{1,0:T(8,128)(2,1)S(1)}, bf16[768,384]{1,0:T(8,128)(2,1)}, u32[]{:S(2)}) copy-start(bf16[768,384]{1,0:T(8,128)(2,1)} %param.7) | copy-start | bytes 1769476
  51.1 1.4 copy-start.1
  68.8 15.4 %collective-permute-start = (bf16[128,768]{0,1:T(8,128)(2,1)S(1)}, bf16[128,768]{0,1:T(8,128)(2,1)S(1)}, u32[]{:S(2)}, u32[]{:S(2)}) collective-permute-start(bf16[128,768]{0,1:T(8,128)(2,1)S(1)} %reduce_sum.43), channel_id=1, source_target_pairs={{0,4},{1,5},{2,6},{3,7},{4,0},{5,1},{6,2},{7,3},{8,12},{9,13},{10,... | collective-permute-start | bytes 589832 | tf_op jit(solution)/shard_map/ppermute | solution.py:68
  120.0 30.9 %all-to-all-start.6 = ((bf16[8,8,896]{2,1,0:T(8,128)(2,1)}), bf16[8,8,896]{2,1,0:T(8,128)(2,1)S(1)}, u32[]{:S(2)}, u32[]{:S(2)}) async-start(bf16[8,8,896]{2,1,0:T(8,128)(2,1)} %bitcast.10), calls=%async_computation.6 | async-start | bytes 229376 | tf_op jit(solution)/shard_map/all_to_all | solution.py:25

commit v2 on v1

--- a/solution.py
+++ b/solution.py
@@ -7,13 +7,16 @@
 
 GELU_SCALE = math.sqrt(2.0 / math.pi)
 BF = jnp.bfloat16
+F16 = jnp.float16
 F32 = jnp.float32
 LANES = 128
+UP_SCALE = 32.0
 
 Y_GROUPS = [[0, 1, 2, 3], [4, 5, 6, 7]]
 X_GROUPS = [[0, 2, 4, 6], [1, 3, 5, 7]]
 CORE_GROUPS = [[0, 1], [2, 3], [4, 5], [6, 7]]
 Z_SWAP = [(i, (i + 4) % 8) for i in range(8)]
+CORE_SWAP = [(i, i ^ 1) for i in range(8)]
 
 
 def spread(block, axis, count, groups=None):
@@ -43,12 +46,19 @@
     got = got.reshape(64, 2 * width + LANES)
     got = spread(got, "row", 4, X_GROUPS)
     got = got.reshape(256, 2 * width + LANES)
-    got = spread(got, "row", 2, CORE_GROUPS)
-    got = got.reshape(512, 2 * width + LANES)
+    rows = spread(got[:, :width], "row", 2, CORE_GROUPS).reshape(512, width)
 
-    rows = got[:, :width]
-    tgrads = got[:, width : 2 * width]
-    sides = got[:, 2 * width :].reshape(64, tok, LANES)
+    up = jnp.dot(rows, w_up, preferred_element_type=F32) * UP_SCALE
+    up = exchange(up.astype(F16).reshape(4, 128, hid), "col", Y_GROUPS)
+    up = jnp.sum(up.astype(F32), axis=0).astype(F16)
+    other = lax.ppermute(up, "col", Z_SWAP)
+
+    own_g = got[:, width:]
+    sib_g = lax.ppermute(own_g, "row", CORE_SWAP)
+    first = lax.axis_index("row") % 2 == 0
+    got_g = jnp.concatenate([jnp.where(first, own_g, sib_g), jnp.where(first, sib_g, own_g)], axis=0)
+    tgrads = got_g[:, :width]
+    sides = got_g[:, width:].reshape(64, tok, LANES)
     pools = sides[:, :pieces, :].reshape(64, width)
     route = sides[:, pieces, :tok].astype(jnp.int32)
     dp_of = lax.broadcasted_iota(jnp.int32, (64, tok), 0) % 8
@@ -59,22 +69,19 @@
     image_grad = (pools.astype(F32) / count).astype(BF)
     returned = jnp.dot(onehot, image_grad, preferred_element_type=F32)
     grads = (tgrads.astype(F32) + returned).astype(BF)
+    back = lax.dot_general(grads, w_down, (((1,), (1,)), ((), ())), preferred_element_type=F32)
 
-    up = jnp.dot(rows, w_up, preferred_element_type=F32)
-    back = lax.dot_general(grads, w_down, (((1,), (1,)), ((), ())), preferred_element_type=F32)
-    both = jnp.concatenate([up.astype(BF), back.astype(BF)], axis=1).reshape(4, 128, 2 * hid)
-    part = exchange(both, "col", Y_GROUPS)
-    part = jnp.sum(part.astype(F32), axis=0).astype(BF)
-    other = lax.ppermute(part, "col", Z_SWAP)
-    total = part.astype(F32) + other.astype(F32)
-    v = total[:, :hid]
+    v = (up.astype(F32) + other.astype(F32)) * (1.0 / UP_SCALE)
     s = jnp.tanh(GELU_SCALE * (v + 0.044715 * v * v * v))
     hidden = (0.5 * v * (1.0 + s)).astype(BF)
     slope = 0.5 * (1.0 + s) + 0.5 * v * (1.0 - s * s) * GELU_SCALE * (1.0 + 3.0 * 0.044715 * v * v)
-    gp = (total[:, hid:] * slope).astype(BF)
-    hg = spread(jnp.concatenate([hidden, gp], axis=1), "col", 4, Y_GROUPS).reshape(512, 2 * hid)
-    hidden = hg[:, :hid]
-    gp = hg[:, hid:]
+
+    mix = jnp.concatenate(
+        [jnp.broadcast_to(hidden[None], (4, 128, hid)), back.astype(BF).reshape(4, 128, hid)], axis=2
+    )
+    mix = exchange(mix, "col", Y_GROUPS)
+    hidden = mix[:, :, :hid].reshape(512, hid)
+    back = jnp.sum(mix[:, :, hid:].astype(F32), axis=0)
 
     down = jnp.dot(hidden, w_down, preferred_element_type=F32)
     pooled_part = (
@@ -85,13 +92,24 @@
     down = down.reshape(2, 4, 64, width + LANES).transpose(1, 0, 2, 3).reshape(8, 64, width + LANES)
     half = exchange(down, "row")
     half = jnp.sum(half.astype(F32), axis=0).astype(BF).reshape(8, tok, width + LANES)
+
+    back_other = lax.ppermute(back.astype(BF), "col", Z_SWAP)
+    gp = ((back + back_other.astype(F32)) * slope).astype(BF)
+    grad_down = lax.dot_general(hidden, grads, (((0,), (0,)), ((), ())), preferred_element_type=F32)
+    half, grad_down = lax.optimization_barrier((half, grad_down))
     last = exchange(half, "dp")
     last = jnp.sum(last.astype(F32), axis=0)
     mixed = last[:, :width].astype(BF)
     pooled = last[:pieces, width:].reshape(1, width)
 
-    grad_down = lax.dot_general(hidden, grads, (((0,), (0,)), ((), ())), preferred_element_type=F32)
-    grad_up = lax.dot_general(rows, gp, (((0,), (0,)), ((), ())), preferred_element_type=F32)
+    y = lax.axis_index("col") % 4
+    gps = [gp] + [
+        lax.ppermute(gp, "col", [(i, i // 4 * 4 + (i - k) % 4) for i in range(8)]) for k in (1, 2, 3)
+    ]
+    turned = lax.dynamic_slice(jnp.concatenate([rows, rows], axis=0), (y * 128, 0), (512, width))
+    grad_up = lax.dot_general(
+        turned, jnp.concatenate(gps, axis=0), (((0,), (0,)), ((), ())), preferred_element_type=F32
+    )
     return (mixed, pooled, grad_up, grad_down)
 
 

time: 153 us -> 147 us (0.961)
  blocking collectives: 83.3 us -> 57.9 us
  starting transfers between devices: 32.7 us -> 54.2 us
  waiting for transfers between devices: 21.8 us -> 17.7 us
    all_to_all x2 -> x1, blocking collectives: 38.1 us -> 11.6 us  [exchange(): lax.all_to_all(blocks, axis, split_axis=0, concat_axis=0, tiled=True, axi...]
    ppermute x1 -> x6, starting transfers between devices: 7.95 us -> 27.6 us  [the longest x1 8.66 us: local(): back_other = lax.ppermute(back.astype(BF), 'col', Z_SWAP)]
    all_to_all x1 -> x0, waiting for transfers between devices: 8.51 us -> none  [spread(): lax.all_to_all(copies, axis, split_axis=0, concat_axis=0, tiled=True, axi...]
    all_to_all x1 -> x3, starting transfers between devices: 20.7 us -> 26.6 us  [exchange(): lax.all_to_all(blocks, axis, split_axis=0, concat_axis=0, tiled=True, axi...]
    all_to_all x1 -> x0, starting transfers between devices: 4.01 us -> none  [spread(): lax.all_to_all(copies, axis, split_axis=0, concat_axis=0, tiled=True, axi...]
    ppermute x1 -> x6, waiting for transfers between devices: 7.42 us -> 9.71 us  [the longest x1 6.16 us: local(): other = lax.ppermute(up, 'col', Z_SWAP)]
    all_to_all x1 -> x3, waiting for transfers between devices: 5.91 us -> 8.03 us  [exchange(): lax.all_to_all(blocks, axis, split_axis=0, concat_axis=0, tiled=True, axi...]
  transfers between devices with their start and end apart: 3 -> 9, of which waited for: 3 -> 5; matrix products, arithmetic and copies ran while one was open for 3% -> 3% of each run, Pallas kernels for 0% -> 0%
where the time goes in v2:
time: 147 us; the launch traced here: 145 us
  blocking collectives  57.9 us (39%)
  starting transfers between devices  54.2 us (37%)
  waiting for transfers between devices  17.7 us (12%)
  matrix products  6.76 us (5%)
  other arithmetic  4 us (3%)
  local copies, waits for them, and re-layouts  3.95 us (3%)
    all_to_all x3, blocking collectives, spread(): lax.all_to_all(copies, axis, split_axis=0, concat_axis=0, tiled=True, axi...  46.3 us
    all_to_all x3, starting transfers between devices, exchange(): lax.all_to_all(blocks, axis, split_axis=0, concat_axis=0, tiled=True, axi...  26.6 us
    all_to_all x1, blocking collectives, exchange(): lax.all_to_all(blocks, axis, split_axis=0, concat_axis=0, tiled=True, axi...  11.6 us
    ppermute x1, starting transfers between devices, local(): back_other = lax.ppermute(back.astype(BF), 'col', Z_SWAP)  8.66 us
    ppermute x3, starting transfers between devices, local(): lax.ppermute(gp, 'col', [(i, i // 4 * 4 + (i - k) % 4) for i in range(8)])  8.42 us
    all_to_all x3, waiting for transfers between devices, exchange(): lax.all_to_all(blocks, axis, split_axis=0, concat_axis=0, tiled=True, axi...  8.03 us
    ppermute x1, starting transfers between devices, local(): other = lax.ppermute(up, 'col', Z_SWAP)  7.94 us
    ppermute x1, waiting for transfers between devices, local(): other = lax.ppermute(up, 'col', Z_SWAP)  6.16 us
  transfers between devices with their start and end apart: 9, of which 5 were waited for; matrix products, arithmetic and copies ran while one was open for 3% of the time, Pallas kernels for 0%

profile of v2, /device:TPU:1, one launch (start us, length us, event | category | flops | bytes accessed | tf_op | source)
XLA Modules:
  0.0 145.5 jit_solution(12984795601142282046)
XLA Ops:
  0.6 0.7 convert_bitcast_fusion
  1.4 0.7 reduce.1
  2.1 0.7 fusion.31
  2.8 24.2 %all_to_all.35 = bf16[8,8,1664]{2,1,0:T(8,128)(2,1)S(1)} all-to-all(bf16[8,8,1664]{2,1,0:T(8,128)(2,1)S(1)} %broadcast_in_dim.16), channel_id=1, replica_groups=mesh['dp'=8,'row'=8,'col'=8] {'dp'}, dimensions={0} | all-to-all | bytes 425984 | tf_op jit(solution)/shard_map/all_to_all | solution.py:24
  27.1 12.5 %all_to_all.36 = bf16[4,64,1664]{2,1,0:T(8,128)(2,1)S(1)} all-to-all(bf16[4,64,1664]{2,1,0:T(8,128)(2,1)S(1)} %broadcast_in_dim.36), channel_id=1, replica_groups={{0,16,32,48},{8,24,40,56},{1,17,33,49},{9,25,41,57},{2,18,34,50},{10,26..., dimensions={0} | all-to-all | bytes 1703936 | tf_op jit(solution)/shard_map/all_to_all | solution.py:24
  39.8 9.5 %all_to_all.37 = bf16[2,256,768]{2,1,0:T(8,128)(2,1)S(1)} all-to-all(bf16[2,256,768]{2,1,0:T(8,128)(2,1)S(1)} %broadcast_in_dim.37), channel_id=1, replica_groups={{0,8},{16,24},{32,40},{48,56},{1,9},{17,25},{33,41},{49,57},{2,10},{18,..., dimensions={0} | all-to-all | bytes 1572864 | tf_op jit(solution)/shard_map/all_to_all | solution.py:24
  49.3 0.9 copy-done.1
  50.2 1.3 fusion
  51.5 4.2 %all-to-all-start.3 = ((f16[4,128,384]{2,1,0:T(8,128)(2,1)}), f16[4,128,384]{2,1,0:T(8,128)(2,1)S(1)}, u32[]{:S(2)}, u32[]{:S(2)}) async-start(f16[4,128,384]{2,1,0:T(8,128)(2,1)} %bitcast.4), calls=%async_computation.3 | async-start | bytes 786432 | tf_op jit(solution)/shard_map/all_to_all | solution.py:28
  55.7 2.6 %collective-permute-start.1 = (bf16[256,896]{1,0:T(8,128)(2,1)S(1)}, bf16[256,896]{1,0:T(8,128)(2,1)S(1)}, u32[]{:S(2)}, u32[]{:S(2)}) collective-permute-start(bf16[256,896]{1,0:T(8,128)(2,1)S(1)} %slice.42), channel_id=1, source_target_pairs={{0,8},{8,0},{16,24},{24,16},{32,40},{40,32},{48,56},{56,48},{1,9},... | collective-permute-start | bytes 1376264 | tf_op jit(solution)/shard_map/ppermute | solution.py:57
  58.3 4.6 %all-to-all-done.3 = f16[4,128,384]{2,1,0:T(8,128)(2,1)S(1)} async-done(((f16[4,128,384]{2,1,0:T(8,128)(2,1)}), f16[4,128,384]{2,1,0:T(8,128)(2,1)S(1)}, u32[]{:S(2)}, u32[]{:S(2)}) %all-to-all-start.3) | async-done | bytes 393248 | tf_op jit(solution)/shard_map/all_to_all | solution.py:28
  63.0 7.9 %collective-permute-start = (f16[128,384]{1,0:T(8,128)(2,1)S(1)}, f16[128,384]{1,0:T(8,128)(2,1)S(1)}, u32[]{:S(2)}, u32[]{:S(2)}) collective-permute-start(f16[128,384]{1,0:T(8,128)(2,1)S(1)} %convert_element_type.87), channel_id=1, source_target_pairs={{0,4},{1,5},{2,6},{3,7},{4,0},{5,1},{6,2},{7,3},{8,12},{9,13},{10,... | collective-permute-start | bytes 294920 | tf_op jit(solution)/shard_map/ppermute | solution.py:54
  71.1 6.2 %collective-permute-done = f16[128,384]{1,0:T(8,128)(2,1)S(1)} collective-permute-done((f16[128,384]{1,0:T(8,128)(2,1)S(1)}, f16[128,384]{1,0:T(8,128)(2,1)S(1)}, u32[]{:S(2)}, u32[]{:S(2)}) %collective-permute-start) | collective-permute-done | bytes 98336 | tf_op jit(solution)/shard_map/ppermute | solution.py:54
  77.9 0.4 add_convert_fusion
  78.4 0.6 convolution_convert_fusion.1
  79.3 11.6 %all_to_all.38 = bf16[4,128,768]{2,1,0:T(8,128)(2,1)S(1)} all-to-all(bf16[4,128,768]{2,1,0:T(8,128)(2,1)S(1)} %pad_maximum_fusion.1), channel_id=1, replica_groups={{0,1,2,3},{4,5,6,7},{8,9,10,11},{12,13,14,15},{16,17,18,19},{20,21,22,2..., dimensions={0} | all-to-all | bytes 1572864 | tf_op jit(solution)/shard_map/all_to_all | solution.py:28
  91.0 0.6 convolution_convert_fusion
  92.1 1.0 copy.14
  93.1 7.5 %all-to-all-start.5 = ((bf16[8,64,896]{2,1,0:T(8,128)(2,1)}), bf16[8,64,896]{2,1,0:T(8,128)(2,1)S(1)}, u32[]{:S(2)}, u32[]{:S(2)}) async-start(bf16[8,64,896]{2,1,0:T(8,128)(2,1)} %bitcast.11), calls=%async_computation.5 | async-start | bytes 1835008 | tf_op jit(solution)/shard_map/all_to_all | solution.py:28
  100.6 8.7 %collective-permute-start.2 = (bf16[128,384]{1,0:T(8,128)(2,1)S(1)}, bf16[128,384]{1,0:T(8,128)(2,1)S(1)}, u32[]{:S(2)}, u32[]{:S(2)}) collective-permute-start(bf16[128,384]{1,0:T(8,128)(2,1)S(1)} %convert_element_type.105), channel_id=1, source_target_pairs={{0,4},{1,5},{2,6},{3,7},{4,0},{5,1},{6,2},{7,3},{8,12},{9,13},{10,... | collective-permute-start | bytes 294920 | tf_op jit(solution)/shard_map/ppermute | solution.py:96
  109.3 1.5 %fusion.40 = f32[384,768]{1,0:T(8,128)} fusion(bf16[512,384]{1,0:T(8,128)(2,1)S(1)} %bitcast.42, bf16[512,768]{1,0:T(8,128)(2,1)S(1)} %copy-done.4), kind=kOutput, calls=%fused_computation.82 | convolution fusion | flops 301989888 | bytes 2359296 | tf_op jit(solution)/shard_map/dot_general | solution.py:98
  110.8 3.4 %all-to-all-done.5 = bf16[8,64,896]{2,1,0:T(8,128)(2,1)S(1)} async-done(((bf16[8,64,896]{2,1,0:T(8,128)(2,1)}), bf16[8,64,896]{2,1,0:T(8,128)(2,1)S(1)}, u32[]{:S(2)}, u32[]{:S(2)}) %all-to-all-start.5) | async-done | bytes 917536 | tf_op jit(solution)/shard_map/all_to_all | solution.py:28
  114.3 0.8 reduce_sum.50
  115.1 14.9 %all-to-all-start.6 = ((bf16[8,8,896]{2,1,0:T(8,128)(2,1)}), bf16[8,8,896]{2,1,0:T(8,128)(2,1)S(1)}, u32[]{:S(2)}, u32[]{:S(2)}) async-start(bf16[8,8,896]{2,1,0:T(8,128)(2,1)} %bitcast.12), calls=%async_computation.6 | async-start | bytes 229376 | tf_op jit(solution)/shard_map/all_to_all | solution.py:28
  130.2 2.2 %collective-permute-start.5 = (bf16[128,384]{1,0:T(8,128)(2,1)S(1)}, bf16[128,384]{1,0:T(8,128)(2,1)S(1)}, u32[]{:S(2)}, u32[]{:S(2)}) collective-permute-start(bf16[128,384]{1,0:T(8,128)(2,1)S(1)} %multiply_convert_fusion), channel_id=1, source_target_pairs={{0,1},{1,2},{2,3},{3,0},{4,5},{5,6},{6,7},{7,4},{8,9},{9,10},{10,1... | collective-permute-start | bytes 294920 | tf_op jit(solution)/shard_map/ppermute | solution.py:107
  132.4 3.7 %collective-permute-start.4 = (bf16[128,384]{1,0:T(8,128)(2,1)S(1)}, bf16[128,384]{1,0:T(8,128)(2,1)S(1)}, u32[]{:S(2)}, u32[]{:S(2)}) collective-permute-start(bf16[128,384]{1,0:T(8,128)(2,1)S(1)} %multiply_convert_fusion), channel_id=1, source_target_pairs={{0,2},{1,3},{2,0},{3,1},{4,6},{5,7},{6,4},{7,5},{8,10},{9,11},{10,... | collective-permute-start | bytes 294920 | tf_op jit(solution)/shard_map/ppermute | solution.py:107
  136.1 2.5 %collective-permute-start.3 = (bf16[128,384]{1,0:T(8,128)(2,1)S(1)}, bf16[128,384]{1,0:T(8,128)(2,1)S(1)}, u32[]{:S(2)}, u32[]{:S(2)}) collective-permute-start(bf16[128,384]{1,0:T(8,128)(2,1)S(1)} %multiply_convert_fusion), channel_id=1, source_target_pairs={{0,3},{1,0},{2,1},{3,2},{4,7},{5,4},{6,5},{7,6},{8,11},{9,8},{10,9... | collective-permute-start | bytes 294920 | tf_op jit(solution)/shard_map/ppermute | solution.py:107
  138.6 0.9 collective-permute-done.4
  139.6 2.6 %collective-permute-done.3 = bf16[128,384]{1,0:T(8,128)(2,1)S(1)} collective-permute-done((bf16[128,384]{1,0:T(8,128)(2,1)S(1)}, bf16[128,384]{1,0:T(8,128)(2,1)S(1)}, u32[]{:S(2)}, u32[]{:S(2)}) %collective-permute-start.3) | collective-permute-done | bytes 98336 | tf_op jit(solution)/shard_map/ppermute | solution.py:107
  142.2 2.1 %fusion.4 = f32[768,384]{1,0:T(8,128)} fusion(s32[]{:T(128)S(6)} %select_n.65, bf16[512,768]{1,0:T(8,128)(2,1)S(1)} %bitcast.46, bf16[128,384]{1,0:T(8,128)(2,1)S(1)} %collective-permute-done.5, bf16[128,384]{1,0:T(8,128)(2,1)S(1)} %collective-permute-done.4, bf16[128,384]{1,0:T(8,128)(2,1)S(1)} %collective-permute-done.3, ...), kind=kOutput, calls=%fused_computation.14 | convolution fusion | flops 305135616 | bytes 2359300 | tf_op jit(solution)/shard_map/dot_general | solution.py:110
  144.3 0.6 slice.68
  144.9 0.6 copy.20
  (48 shorter events, 2.2 us)
Async XLA Ops:
  0.6 77.7 %copy-start = (bf16[384,768]{1,0:T(8,128)(2,1)S(1)}, bf16[384,768]{1,0:T(8,128)(2,1)}, u32[]{:S(2)}) copy-start(bf16[384,768]{1,0:T(8,128)(2,1)} %param.8) | copy-start | bytes 1769476
  39.7 10.5 %copy-start.5 = (bf16[768,384]{1,0:T(8,128)(2,1)S(1)}, bf16[768,384]{1,0:T(8,128)(2,1)}, u32[]{:S(2)}) copy-start(bf16[768,384]{1,0:T(8,128)(2,1)} %param.7) | copy-start | bytes 1769476
  49.3 0.9 copy-start.1
  51.5 11.4 %all-to-all-start.3 = ((f16[4,128,384]{2,1,0:T(8,128)(2,1)}), f16[4,128,384]{2,1,0:T(8,128)(2,1)S(1)}, u32[]{:S(2)}, u32[]{:S(2)}) async-start(f16[4,128,384]{2,1,0:T(8,128)(2,1)} %bitcast.4), calls=%async_computation.3 | async-start | bytes 786432 | tf_op jit(solution)/shard_map/all_to_all | solution.py:28
  55.7 21.6 %collective-permute-start.1 = (bf16[256,896]{1,0:T(8,128)(2,1)S(1)}, bf16[256,896]{1,0:T(8,128)(2,1)S(1)}, u32[]{:S(2)}, u32[]{:S(2)}) collective-permute-start(bf16[256,896]{1,0:T(8,128)(2,1)S(1)} %slice.42), channel_id=1, source_target_pairs={{0,8},{8,0},{16,24},{24,16},{32,40},{40,32},{48,56},{56,48},{1,9},... | collective-permute-start | bytes 1376264 | tf_op jit(solution)/shard_map/ppermute | solution.py:57
  63.0 14.3 %collective-permute-start = (f16[128,384]{1,0:T(8,128)(2,1)S(1)}, f16[128,384]{1,0:T(8,128)(2,1)S(1)}, u32[]{:S(2)}, u32[]{:S(2)}) collective-permute-start(f16[128,384]{1,0:T(8,128)(2,1)S(1)} %convert_element_type.87), channel_id=1, source_target_pairs={{0,4},{1,5},{2,6},{3,7},{4,0},{5,1},{6,2},{7,3},{8,12},{9,13},{10,... | collective-permute-start | bytes 294920 | tf_op jit(solution)/shard_map/ppermute | solution.py:54
  78.3 0.9 copy-start.3
  93.1 21.2 %all-to-all-start.5 = ((bf16[8,64,896]{2,1,0:T(8,128)(2,1)}), bf16[8,64,896]{2,1,0:T(8,128)(2,1)S(1)}, u32[]{:S(2)}, u32[]{:S(2)}) async-start(bf16[8,64,896]{2,1,0:T(8,128)(2,1)} %bitcast.11), calls=%async_computation.5 | async-start | bytes 1835008 | tf_op jit(solution)/shard_map/all_to_all | solution.py:28
  100.6 8.7 %copy-start.4 = (bf16[512,768]{1,0:T(8,128)(2,1)S(1)}, bf16[512,768]{1,0:T(8,128)(2,1)}, u32[]{:S(2)}) copy-start(bf16[512,768]{1,0:T(8,128)(2,1)} %copy-done.3) | copy-start | bytes 2359300
  100.6 29.4 %collective-permute-start.2 = (bf16[128,384]{1,0:T(8,128)(2,1)S(1)}, bf16[128,384]{1,0:T(8,128)(2,1)S(1)}, u32[]{:S(2)}, u32[]{:S(2)}) collective-permute-start(bf16[128,384]{1,0:T(8,128)(2,1)S(1)} %convert_element_type.105), channel_id=1, source_target_pairs={{0,4},{1,5},{2,6},{3,7},{4,0},{5,1},{6,2},{7,3},{8,12},{9,13},{10,... | collective-permute-start | bytes 294920 | tf_op jit(solution)/shard_map/ppermute | solution.py:96
  110.8 31.4 %copy-start.2 = (bf16[2,256,768]{2,1,0:T(8,128)(2,1)S(1)}, bf16[2,256,768]{2,1,0:T(8,128)(2,1)}, u32[]{:S(2)}) copy-start(bf16[2,256,768]{2,1,0:T(8,128)(2,1)} %copy-done.1) | copy-start | bytes 2359300
  115.1 29.2 %all-to-all-start.6 = ((bf16[8,8,896]{2,1,0:T(8,128)(2,1)}), bf16[8,8,896]{2,1,0:T(8,128)(2,1)S(1)}, u32[]{:S(2)}, u32[]{:S(2)}) async-start(bf16[8,8,896]{2,1,0:T(8,128)(2,1)} %bitcast.12), calls=%async_computation.6 | async-start | bytes 229376 | tf_op jit(solution)/shard_map/all_to_all | solution.py:28
  130.2 8.5 %collective-permute-start.5 = (bf16[128,384]{1,0:T(8,128)(2,1)S(1)}, bf16[128,384]{1,0:T(8,128)(2,1)S(1)}, u32[]{:S(2)}, u32[]{:S(2)}) collective-permute-start(bf16[128,384]{1,0:T(8,128)(2,1)S(1)} %multiply_convert_fusion), channel_id=1, source_target_pairs={{0,1},{1,2},{2,3},{3,0},{4,5},{5,6},{6,7},{7,4},{8,9},{9,10},{10,1... | collective-permute-start | bytes 294920 | tf_op jit(solution)/shard_map/ppermute | solution.py:107
  132.4 7.2 %collective-permute-start.4 = (bf16[128,384]{1,0:T(8,128)(2,1)S(1)}, bf16[128,384]{1,0:T(8,128)(2,1)S(1)}, u32[]{:S(2)}, u32[]{:S(2)}) collective-permute-start(bf16[128,384]{1,0:T(8,128)(2,1)S(1)} %multiply_convert_fusion), channel_id=1, source_target_pairs={{0,2},{1,3},{2,0},{3,1},{4,6},{5,7},{6,4},{7,5},{8,10},{9,11},{10,... | collective-permute-start | bytes 294920 | tf_op jit(solution)/shard_map/ppermute | solution.py:107
  136.1 6.1 %collective-permute-start.3 = (bf16[128,384]{1,0:T(8,128)(2,1)S(1)}, bf16[128,384]{1,0:T(8,128)(2,1)S(1)}, u32[]{:S(2)}, u32[]{:S(2)}) collective-permute-start(bf16[128,384]{1,0:T(8,128)(2,1)S(1)} %multiply_convert_fusion), channel_id=1, source_target_pairs={{0,3},{1,0},{2,1},{3,2},{4,7},{5,4},{6,5},{7,6},{8,11},{9,8},{10,9... | collective-permute-start | bytes 294920 | tf_op jit(solution)/shard_map/ppermute | solution.py:107

commit v3 on v2

--- a/solution.py
+++ b/solution.py
@@ -24,6 +24,10 @@
     return lax.all_to_all(copies, axis, split_axis=0, concat_axis=0, tiled=True, axis_index_groups=groups)
 
 
+def gather(block, axis, groups):
+    return lax.all_gather(block, axis, axis=0, tiled=True, axis_index_groups=groups)
+
+
 def exchange(blocks, axis, groups=None):
     return lax.all_to_all(blocks, axis, split_axis=0, concat_axis=0, tiled=True, axis_index_groups=groups)
 
@@ -44,19 +48,17 @@
     block = jnp.concatenate([patches, tok_grad, side], axis=1)
     got = spread(block, "dp", 8)
     got = got.reshape(64, 2 * width + LANES)
-    got = spread(got, "row", 4, X_GROUPS)
-    got = got.reshape(256, 2 * width + LANES)
-    rows = spread(got[:, :width], "row", 2, CORE_GROUPS).reshape(512, width)
+    got = gather(got, "row", X_GROUPS)
+    rows = gather(got[:, :width], "row", CORE_GROUPS)
 
     up = jnp.dot(rows, w_up, preferred_element_type=F32) * UP_SCALE
-    up = exchange(up.astype(F16).reshape(4, 128, hid), "col", Y_GROUPS)
+    up = up.astype(F16)
+    up = exchange(up.reshape(4, 128, hid), "col", Y_GROUPS)
     up = jnp.sum(up.astype(F32), axis=0).astype(F16)
     other = lax.ppermute(up, "col", Z_SWAP)
+    own_g, _ = lax.optimization_barrier((got[:, width:], up))
 
-    own_g = got[:, width:]
-    sib_g = lax.ppermute(own_g, "row", CORE_SWAP)
-    first = lax.axis_index("row") % 2 == 0
-    got_g = jnp.concatenate([jnp.where(first, own_g, sib_g), jnp.where(first, sib_g, own_g)], axis=0)
+    got_g = gather(own_g, "row", CORE_GROUPS)
     tgrads = got_g[:, :width]
     sides = got_g[:, width:].reshape(64, tok, LANES)
     pools = sides[:, :pieces, :].reshape(64, width)
@@ -89,8 +91,15 @@
     )
     packed = jnp.pad(pooled_part.astype(BF).reshape(64, pieces, LANES), ((0, 0), (0, tok - pieces), (0, 0)))
     down = jnp.concatenate([down.astype(BF), packed.reshape(512, LANES)], axis=1)
-    down = down.reshape(2, 4, 64, width + LANES).transpose(1, 0, 2, 3).reshape(8, 64, width + LANES)
-    half = exchange(down, "row")
+    down = down.reshape(2, 256, width + LANES)
+    core = lax.axis_index("row") % 2
+    sent = lax.dynamic_index_in_dim(down, 1 - core, 0, keepdims=False)
+    sent = gather(sent, "row", CORE_GROUPS).reshape(2, 256, width + LANES)
+    half = lax.dynamic_index_in_dim(down, core, 0).astype(F32)
+    half = half + lax.dynamic_index_in_dim(sent, 1 - core, 0).astype(F32)
+    half = half.astype(BF).reshape(4, 64, width + LANES)
+    back, _ = lax.optimization_barrier((back, half))
+    half = exchange(half, "row", X_GROUPS)
     half = jnp.sum(half.astype(F32), axis=0).astype(BF).reshape(8, tok, width + LANES)
 
     back_other = lax.ppermute(back.astype(BF), "col", Z_SWAP)

time: 147 us -> 143 us (0.973)
  the two profiles are of different devices: /device:TPU:1 before, /device:TPU:66 now
where the time goes in v3:
time: 143 us
  starting transfers between devices  59.8 us (42%)
  waiting for transfers between devices  43.2 us (30%)
  blocking collectives  20.9 us (15%)
  matrix products  7.41 us (5%)
  other arithmetic  5.52 us (4%)
  local copies, waits for them, and re-layouts  4.83 us (3%)
    all_to_all x4, starting transfers between devices, exchange(): lax.all_to_all(blocks, axis, split_axis=0, concat_axis=0, tiled=True, axi...  22.9 us
    all_gather x4, blocking collectives, gather(): lax.all_gather(block, axis, axis=0, tiled=True, axis_index_groups=groups)  20.9 us
    all_to_all x4, waiting for transfers between devices, exchange(): lax.all_to_all(blocks, axis, split_axis=0, concat_axis=0, tiled=True, axi...  17.6 us
    all_to_all x1, waiting for transfers between devices, spread(): lax.all_to_all(copies, axis, split_axis=0, concat_axis=0, tiled=True, axi...  13.1 us
    all_to_all x1, starting transfers between devices, spread(): lax.all_to_all(copies, axis, split_axis=0, concat_axis=0, tiled=True, axi...  12.2 us
    ppermute x3, starting transfers between devices, local(): lax.ppermute(gp, 'col', [(i, i // 4 * 4 + (i - k) % 4) for i in range(8)])  8.98 us
    ppermute x1, starting transfers between devices, local(): other = lax.ppermute(up, 'col', Z_SWAP)  8.22 us
    ppermute x1, starting transfers between devices, local(): back_other = lax.ppermute(back.astype(BF), 'col', Z_SWAP)  7.5 us
  transfers between devices with their start and end apart: 10, of which 7 were waited for; matrix products, arithmetic and copies ran while one was open for 4% of the time, Pallas kernels for 0%

profile of v3, /device:TPU:66, one launch (start us, length us, event | category | flops | bytes accessed | tf_op | source)
XLA Modules:
  0.0 142.6 jit_solution(8723012752488545351)
XLA Ops:
  0.6 0.7 convert_bitcast_fusion
  2.1 0.7 fusion.30
  3.5 12.2 %all-to-all-start = ((bf16[8,8,1664]{2,1,0:T(8,128)(2,1)}), bf16[8,8,1664]{2,1,0:T(8,128)(2,1)S(1)}, u32[]{:S(2)}, u32[]{:S(2)}) async-start(bf16[8,8,1664]{2,1,0:T(8,128)(2,1)} %broadcast_in_dim.10), calls=%async_computation | async-start | bytes 425984 | tf_op jit(solution)/shard_map/all_to_all | solution.py:24
  15.7 13.1 %all-to-all-done = bf16[8,8,1664]{2,1,0:T(8,128)(2,1)S(1)} async-done(((bf16[8,8,1664]{2,1,0:T(8,128)(2,1)}), bf16[8,8,1664]{2,1,0:T(8,128)(2,1)S(1)}, u32[]{:S(2)}, u32[]{:S(2)}) %all-to-all-start) | async-done | bytes 213024 | tf_op jit(solution)/shard_map/all_to_all | solution.py:24
  28.8 13.5 %all_gather.12 = bf16[256,1664]{1,0:T(8,128)(2,1)S(1)} all-gather(bf16[64,1664]{1,0:T(8,128)(2,1)S(1)} %bitcast.42), channel_id=1, replica_groups={{0,16,32,48},{8,24,40,56},{1,17,33,49},{9,25,41,57},{2,18,34,50},{10,26..., dimensions={0}, use_global_device_ids=true | all-gather | bytes 1064960 | tf_op jit(solution)/shard_map/all_gather | solution.py:28
  42.3 2.5 %all_gather.13 = bf16[512,768]{1,0:T(8,128)(2,1)S(1)} all-gather(bf16[256,768]{1,0:T(8,128)(2,1)S(1)} %slice.41), channel_id=1, replica_groups={{0,8},{16,24},{32,40},{48,56},{1,9},{17,25},{33,41},{49,57},{2,10},{18,..., dimensions={0}, use_global_device_ids=true | all-gather | bytes 1179648 | tf_op jit(solution)/shard_map/all_gather | solution.py:28
  44.8 1.3 fusion
  46.1 4.5 %all-to-all-start.1 = ((f16[4,128,384]{2,1,0:T(8,128)(2,1)}), f16[4,128,384]{2,1,0:T(8,128)(2,1)S(1)}, u32[]{:S(2)}, u32[]{:S(2)}) async-start(f16[4,128,384]{2,1,0:T(8,128)(2,1)} %bitcast.2), calls=%async_computation.1 | async-start | bytes 786432 | tf_op jit(solution)/shard_map/all_to_all | solution.py:32
  50.8 8.2 %all-to-all-done.1 = f16[4,128,384]{2,1,0:T(8,128)(2,1)S(1)} async-done(((f16[4,128,384]{2,1,0:T(8,128)(2,1)}), f16[4,128,384]{2,1,0:T(8,128)(2,1)S(1)}, u32[]{:S(2)}, u32[]{:S(2)}) %all-to-all-start.1) | async-done | bytes 393248 | tf_op jit(solution)/shard_map/all_to_all | solution.py:32
  59.0 8.2 %collective-permute-start = (f16[128,384]{1,0:T(8,128)(2,1)S(1)}, f16[128,384]{1,0:T(8,128)(2,1)S(1)}, u32[]{:S(2)}, u32[]{:S(2)}) collective-permute-start(f16[128,384]{1,0:T(8,128)(2,1)S(1)} %convert_element_type.96), channel_id=1, source_target_pairs={{0,4},{1,5},{2,6},{3,7},{4,0},{5,1},{6,2},{7,3},{8,12},{9,13},{10,... | collective-permute-start | bytes 294920 | tf_op jit(solution)/shard_map/ppermute | solution.py:58
  67.3 2.5 %all_gather.14 = bf16[512,896]{1,0:T(8,128)(2,1)S(1)} all-gather(bf16[256,896]{1,0:T(8,128)(2,1)S(1)} %slice-done), channel_id=1, replica_groups={{0,8},{16,24},{32,40},{48,56},{1,9},{17,25},{33,41},{49,57},{2,10},{18,..., dimensions={0}, use_global_device_ids=true | all-gather | bytes 1376256 | tf_op jit(solution)/shard_map/all_gather | solution.py:28
  71.2 6.2 %collective-permute-done = f16[128,384]{1,0:T(8,128)(2,1)S(1)} collective-permute-done((f16[128,384]{1,0:T(8,128)(2,1)S(1)}, f16[128,384]{1,0:T(8,128)(2,1)S(1)}, u32[]{:S(2)}, u32[]{:S(2)}) %collective-permute-start) | collective-permute-done | bytes 98336 | tf_op jit(solution)/shard_map/ppermute | solution.py:58
  77.6 0.9 pad_maximum_fusion
  78.6 3.5 %all-to-all-start.2 = ((bf16[4,128,768]{2,1,0:T(8,128)(2,1)}), bf16[4,128,768]{2,1,0:T(8,128)(2,1)S(1)}, u32[]{:S(2)}, u32[]{:S(2)}) async-start(bf16[4,128,768]{2,1,0:T(8,128)(2,1)} %pad_maximum_fusion), calls=%async_computation.2 | async-start | bytes 1572864 | tf_op jit(solution)/shard_map/all_to_all | solution.py:32
  82.1 9.4 %all-to-all-done.2 = bf16[4,128,768]{2,1,0:T(8,128)(2,1)S(1)} async-done(((bf16[4,128,768]{2,1,0:T(8,128)(2,1)}), bf16[4,128,768]{2,1,0:T(8,128)(2,1)S(1)}, u32[]{:S(2)}, u32[]{:S(2)}) %all-to-all-start.2) | async-done | bytes 786464 | tf_op jit(solution)/shard_map/all_to_all | solution.py:32
  92.1 0.9 fusion.1
  93.0 1.7 %reshape.126 = bf16[64,6,128]{2,1,0:T(8,128)(2,1)} reshape(bf16[64,768]{1,0:T(8,128)(2,1)} %fusion.1) | data formatting | bytes 196608 | tf_op jit(solution)/shard_map/reshape | solution.py:92
  94.7 0.9 pad.9
  95.7 2.5 %all-gather = bf16[1,512,896]{2,1,0:T(8,128)(2,1)S(1)} all-gather(bf16[1,256,896]{2,1,0:T(8,128)(2,1)S(1)} %fusion.5), channel_id=2, replica_groups={{0,8},{16,24},{32,40},{48,56},{1,9},{17,25},{33,41},{49,57},{2,10},{18,..., dimensions={1}, use_global_device_ids=true | all-gather | bytes 1376256 | tf_op jit(solution)/shard_map/all_gather | solution.py:28
  98.1 0.9 add_convert_fusion.1
  99.0 10.3 %all-to-all-start.3 = ((bf16[4,64,896]{2,1,0:T(8,128)(2,1)}), bf16[4,64,896]{2,1,0:T(8,128)(2,1)S(1)}, u32[]{:S(2)}, u32[]{:S(2)}) async-start(bf16[4,64,896]{2,1,0:T(8,128)(2,1)} %bitcast.9), calls=%async_computation.3 | async-start | bytes 917504 | tf_op jit(solution)/shard_map/all_to_all | solution.py:32
  109.4 7.5 %collective-permute-start.1 = (bf16[128,384]{1,0:T(8,128)(2,1)S(1)}, bf16[128,384]{1,0:T(8,128)(2,1)S(1)}, u32[]{:S(2)}, u32[]{:S(2)}) collective-permute-start(bf16[128,384]{1,0:T(8,128)(2,1)S(1)} %convert_element_type.117), channel_id=1, source_target_pairs={{0,4},{1,5},{2,6},{3,7},{4,0},{5,1},{6,2},{7,3},{8,12},{9,13},{10,... | collective-permute-start | bytes 294920 | tf_op jit(solution)/shard_map/ppermute | solution.py:105
  116.9 1.5 %fusion.39 = f32[384,768]{1,0:T(8,128)} fusion(bf16[512,384]{1,0:T(8,128)(2,1)S(1)} %bitcast.38, bf16[512,768]{1,0:T(8,128)(2,1)S(1)} %copy-done.3), kind=kOutput, calls=%fused_computation.81 | convolution fusion | flops 301989888 | bytes 2359296 | tf_op jit(solution)/shard_map/dot_general | solution.py:107
  118.5 0.7 reduce_sum.50
  119.2 4.6 %all-to-all-start.4 = ((bf16[8,8,896]{2,1,0:T(8,128)(2,1)}), bf16[8,8,896]{2,1,0:T(8,128)(2,1)S(1)}, u32[]{:S(2)}, u32[]{:S(2)}) async-start(bf16[8,8,896]{2,1,0:T(8,128)(2,1)} %bitcast.10), calls=%async_computation.4 | async-start | bytes 229376 | tf_op jit(solution)/shard_map/all_to_all | solution.py:32
  123.8 2.4 %collective-permute-done.1 = bf16[128,384]{1,0:T(8,128)(2,1)S(1)} collective-permute-done((bf16[128,384]{1,0:T(8,128)(2,1)S(1)}, bf16[128,384]{1,0:T(8,128)(2,1)S(1)}, u32[]{:S(2)}, u32[]{:S(2)}) %collective-permute-start.1) | collective-permute-done | bytes 98336 | tf_op jit(solution)/shard_map/ppermute | solution.py:105
  126.3 2.5 %collective-permute-start.4 = (bf16[128,384]{1,0:T(8,128)(2,1)S(1)}, bf16[128,384]{1,0:T(8,128)(2,1)S(1)}, u32[]{:S(2)}, u32[]{:S(2)}) collective-permute-start(bf16[128,384]{1,0:T(8,128)(2,1)S(1)} %multiply_convert_fusion), channel_id=1, source_target_pairs={{0,1},{1,2},{2,3},{3,0},{4,5},{5,6},{6,7},{7,4},{8,9},{9,10},{10,1... | collective-permute-start | bytes 294920 | tf_op jit(solution)/shard_map/ppermute | solution.py:116
  128.8 4.0 %collective-permute-start.3 = (bf16[128,384]{1,0:T(8,128)(2,1)S(1)}, bf16[128,384]{1,0:T(8,128)(2,1)S(1)}, u32[]{:S(2)}, u32[]{:S(2)}) collective-permute-start(bf16[128,384]{1,0:T(8,128)(2,1)S(1)} %multiply_convert_fusion), channel_id=1, source_target_pairs={{0,2},{1,3},{2,0},{3,1},{4,6},{5,7},{6,4},{7,5},{8,10},{9,11},{10,... | collective-permute-start | bytes 294920 | tf_op jit(solution)/shard_map/ppermute | solution.py:116
  132.8 2.5 %collective-permute-start.2 = (bf16[128,384]{1,0:T(8,128)(2,1)S(1)}, bf16[128,384]{1,0:T(8,128)(2,1)S(1)}, u32[]{:S(2)}, u32[]{:S(2)}) collective-permute-start(bf16[128,384]{1,0:T(8,128)(2,1)S(1)} %multiply_convert_fusion), channel_id=1, source_target_pairs={{0,3},{1,0},{2,1},{3,2},{4,7},{5,4},{6,5},{7,6},{8,11},{9,8},{10,9... | collective-permute-start | bytes 294920 | tf_op jit(solution)/shard_map/ppermute | solution.py:116
  135.4 1.5 %collective-permute-done.3 = bf16[128,384]{1,0:T(8,128)(2,1)S(1)} collective-permute-done((bf16[128,384]{1,0:T(8,128)(2,1)S(1)}, bf16[128,384]{1,0:T(8,128)(2,1)S(1)}, u32[]{:S(2)}, u32[]{:S(2)}) %collective-permute-start.3) | collective-permute-done | bytes 98336 | tf_op jit(solution)/shard_map/ppermute | solution.py:116
  136.8 2.5 %collective-permute-done.2 = bf16[128,384]{1,0:T(8,128)(2,1)S(1)} collective-permute-done((bf16[128,384]{1,0:T(8,128)(2,1)S(1)}, bf16[128,384]{1,0:T(8,128)(2,1)S(1)}, u32[]{:S(2)}, u32[]{:S(2)}) %collective-permute-start.2) | collective-permute-done | bytes 98336 | tf_op jit(solution)/shard_map/ppermute | solution.py:116
  139.3 2.1 %fusion.3 = f32[768,384]{1,0:T(8,128)} fusion(s32[]{:T(128)S(6)} %select_n.61, bf16[512,768]{1,0:T(8,128)(2,1)S(1)} %all_gather.13, bf16[128,384]{1,0:T(8,128)(2,1)S(1)} %collective-permute-done.4, bf16[128,384]{1,0:T(8,128)(2,1)S(1)} %collective-permute-done.3, bf16[128,384]{1,0:T(8,128)(2,1)S(1)} %collective-permute-done.2, ...), kind=kOutput, calls=%fused_computation.15 | convolution fusion | flops 305135616 | bytes 2359300 | tf_op jit(solution)/shard_map/dot_general | solution.py:119
  (50 shorter events, 5.4 us)
Async XLA Ops:
  0.6 70.0 %copy-start = (bf16[384,768]{1,0:T(8,128)(2,1)S(1)}, bf16[384,768]{1,0:T(8,128)(2,1)}, u32[]{:S(2)}) copy-start(bf16[384,768]{1,0:T(8,128)(2,1)} %param.8) | copy-start | bytes 1769476
  3.5 25.3 %all-to-all-start = ((bf16[8,8,1664]{2,1,0:T(8,128)(2,1)}), bf16[8,8,1664]{2,1,0:T(8,128)(2,1)S(1)}, u32[]{:S(2)}, u32[]{:S(2)}) async-start(bf16[8,8,1664]{2,1,0:T(8,128)(2,1)} %broadcast_in_dim.10), calls=%async_computation | async-start | bytes 425984 | tf_op jit(solution)/shard_map/all_to_all | solution.py:24
  42.3 8.5 %copy-start.1 = (bf16[256,1664]{1,0:T(8,128)(2,1)}, bf16[256,1664]{1,0:T(8,128)(2,1)S(1)}, u32[]{:S(2)}) copy-start(bf16[256,1664]{1,0:T(8,128)(2,1)S(1)} %all_gather.12) | copy-start | bytes 2555908
  42.3 2.5 %copy-start.6 = (bf16[768,384]{1,0:T(8,128)(2,1)S(1)}, bf16[768,384]{1,0:T(8,128)(2,1)}, u32[]{:S(2)}) copy-start(bf16[768,384]{1,0:T(8,128)(2,1)} %param.7) | copy-start | bytes 1769476
  46.1 12.8 %all-to-all-start.1 = ((f16[4,128,384]{2,1,0:T(8,128)(2,1)}), f16[4,128,384]{2,1,0:T(8,128)(2,1)S(1)}, u32[]{:S(2)}, u32[]{:S(2)}) async-start(f16[4,128,384]{2,1,0:T(8,128)(2,1)} %bitcast.2), calls=%async_computation.1 | async-start | bytes 786432 | tf_op jit(solution)/shard_map/all_to_all | solution.py:32
  50.8 16.5 %slice-start = ((bf16[256,1664]{1,0:T(8,128)(2,1)}), bf16[256,896]{1,0:T(8,128)(2,1)S(1)}, s32[]{:S(2)}) async-start(bf16[256,1664]{1,0:T(8,128)(2,1)} %copy-done.1), calls=%async_computation.5 | async-start | bytes 917504 | tf_op jit(solution)/shard_map/slice | solution.py:59
  59.0 18.4 %collective-permute-start = (f16[128,384]{1,0:T(8,128)(2,1)S(1)}, f16[128,384]{1,0:T(8,128)(2,1)S(1)}, u32[]{:S(2)}, u32[]{:S(2)}) collective-permute-start(f16[128,384]{1,0:T(8,128)(2,1)S(1)} %convert_element_type.96), channel_id=1, source_target_pairs={{0,4},{1,5},{2,6},{3,7},{4,0},{5,1},{6,2},{7,3},{8,12},{9,13},{10,... | collective-permute-start | bytes 294920 | tf_op jit(solution)/shard_map/ppermute | solution.py:58
  70.6 7.0 %copy-start.2 = (bf16[512,768]{1,0:T(8,128)(2,1)}, bf16[512,768]{1,0:T(8,128)(2,1)S(1)}, u32[]{:S(2)}) copy-start(bf16[512,768]{1,0:T(8,128)(2,1)S(1)} %add_convert_fusion) | copy-start | bytes 2359300
  77.5 1.1 copy-start.4
  78.6 13.0 %all-to-all-start.2 = ((bf16[4,128,768]{2,1,0:T(8,128)(2,1)}), bf16[4,128,768]{2,1,0:T(8,128)(2,1)S(1)}, u32[]{:S(2)}, u32[]{:S(2)}) async-start(bf16[4,128,768]{2,1,0:T(8,128)(2,1)} %pad_maximum_fusion), calls=%async_computation.2 | async-start | bytes 1572864 | tf_op jit(solution)/shard_map/all_to_all | solution.py:32
  99.0 19.4 %all-to-all-start.3 = ((bf16[4,64,896]{2,1,0:T(8,128)(2,1)}), bf16[4,64,896]{2,1,0:T(8,128)(2,1)S(1)}, u32[]{:S(2)}, u32[]{:S(2)}) async-start(bf16[4,64,896]{2,1,0:T(8,128)(2,1)} %bitcast.9), calls=%async_computation.3 | async-start | bytes 917504 | tf_op jit(solution)/shard_map/all_to_all | solution.py:32
  109.3 7.6 %copy-start.3 = (bf16[512,768]{1,0:T(8,128)(2,1)S(1)}, bf16[512,768]{1,0:T(8,128)(2,1)}, u32[]{:S(2)}) copy-start(bf16[512,768]{1,0:T(8,128)(2,1)} %copy-done.2) | copy-start | bytes 2359300
  109.4 16.8 %copy-start.5 = (f16[128,384]{1,0:T(8,128)(2,1)S(1)}, f16[128,384]{1,0:T(8,128)(2,1)}, u32[]{:S(2)}) copy-start(f16[128,384]{1,0:T(8,128)(2,1)} %copy-done.4) | copy-start | bytes 294916
  109.4 16.8 %collective-permute-start.1 = (bf16[128,384]{1,0:T(8,128)(2,1)S(1)}, bf16[128,384]{1,0:T(8,128)(2,1)S(1)}, u32[]{:S(2)}, u32[]{:S(2)}) collective-permute-start(bf16[128,384]{1,0:T(8,128)(2,1)S(1)} %convert_element_type.117), channel_id=1, source_target_pairs={{0,4},{1,5},{2,6},{3,7},{4,0},{5,1},{6,2},{7,3},{8,12},{9,13},{10,... | collective-permute-start | bytes 294920 | tf_op jit(solution)/shard_map/ppermute | solution.py:105
  119.2 22.2 %all-to-all-start.4 = ((bf16[8,8,896]{2,1,0:T(8,128)(2,1)}), bf16[8,8,896]{2,1,0:T(8,128)(2,1)S(1)}, u32[]{:S(2)}, u32[]{:S(2)}) async-start(bf16[8,8,896]{2,1,0:T(8,128)(2,1)} %bitcast.10), calls=%async_computation.4 | async-start | bytes 229376 | tf_op jit(solution)/shard_map/all_to_all | solution.py:32
  126.3 9.0 %collective-permute-start.4 = (bf16[128,384]{1,0:T(8,128)(2,1)S(1)}, bf16[128,384]{1,0:T(8,128)(2,1)S(1)}, u32[]{:S(2)}, u32[]{:S(2)}) collective-permute-start(bf16[128,384]{1,0:T(8,128)(2,1)S(1)} %multiply_convert_fusion), channel_id=1, source_target_pairs={{0,1},{1,2},{2,3},{3,0},{4,5},{5,6},{6,7},{7,4},{8,9},{9,10},{10,1... | collective-permute-start | bytes 294920 | tf_op jit(solution)/shard_map/ppermute | solution.py:116
  128.8 8.0 %collective-permute-start.3 = (bf16[128,384]{1,0:T(8,128)(2,1)S(1)}, bf16[128,384]{1,0:T(8,128)(2,1)S(1)}, u32[]{:S(2)}, u32[]{:S(2)}) collective-permute-start(bf16[128,384]{1,0:T(8,128)(2,1)S(1)} %multiply_convert_fusion), channel_id=1, source_target_pairs={{0,2},{1,3},{2,0},{3,1},{4,6},{5,7},{6,4},{7,5},{8,10},{9,11},{10,... | collective-permute-start | bytes 294920 | tf_op jit(solution)/shard_map/ppermute | solution.py:116
  132.8 6.5 %collective-permute-start.2 = (bf16[128,384]{1,0:T(8,128)(2,1)S(1)}, bf16[128,384]{1,0:T(8,128)(2,1)S(1)}, u32[]{:S(2)}, u32[]{:S(2)}) collective-permute-start(bf16[128,384]{1,0:T(8,128)(2,1)S(1)} %multiply_convert_fusion), channel_id=1, source_target_pairs={{0,3},{1,0},{2,1},{3,2},{4,7},{5,4},{6,5},{7,6},{8,11},{9,8},{10,9... | collective-permute-start | bytes 294920 | tf_op jit(solution)/shard_map/ppermute | solution.py:116

commit v4 on v3

v4 whole, which is shorter than its diff:
```python
import math

import jax
import jax.numpy as jnp
from jax import lax
from jax.experimental import pallas as pl
from jax.experimental.pallas import tpu as pltpu
from jax.sharding import PartitionSpec as P

GELU_SCALE = math.sqrt(2.0 / math.pi)
BF = jnp.bfloat16
F16 = jnp.float16
F32 = jnp.float32
LANES = 128
UP_SCALE = 32.0

Y_GROUPS = [[0, 1, 2, 3], [4, 5, 6, 7]]
X_GROUPS = [[0, 2, 4, 6], [1, 3, 5, 7]]
CORE_GROUPS = [[0, 1], [2, 3], [4, 5], [6, 7]]
Z_SWAP = [(i, (i + 4) % 8) for i in range(8)]
CORE_SWAP = [(i, i ^ 1) for i in range(8)]


def spread(block, axis, count, groups=None):
    copies = jnp.broadcast_to(block[None], (count,) + block.shape)
    return lax.all_to_all(copies, axis, split_axis=0, concat_axis=0, tiled=True, axis_index_groups=groups)


def gather(block, axis, groups):
    return lax.all_gather(block, axis, axis=0, tiled=True, axis_index_groups=groups)


def exchange(blocks, axis, groups=None):
    return lax.all_to_all(blocks, axis, split_axis=0, concat_axis=0, tiled=True, axis_index_groups=groups)


def pack_kernel(route_ref, patches_ref, tgrad_ref, pool_ref, out_ref):
    width = patches_ref.shape[1]
    pieces = width // LANES
    tok = patches_ref.shape[0]
    lane = lax.broadcasted_iota(jnp.int32, (tok, LANES), 1)
    sub = lax.broadcasted_iota(jnp.int32, (tok, LANES), 0)
    side = jnp.zeros((tok, LANES), F32)
    for j in range(pieces):
        piece = pool_ref[:, j * LANES : (j + 1) * LANES].astype(F32)
        side = jnp.where(sub == j, jnp.broadcast_to(piece, (tok, LANES)), side)
    for t in range(tok):
        side = jnp.where((sub == pieces) & (lane == t), route_ref[t].astype(F32), side)
    side = side.astype(BF)
    for k in range(out_ref.shape[0]):
        out_ref[k, :, :width] = patches_ref[...]
        out_ref[k, :, width : 2 * width] = tgrad_ref[...]
        out_ref[k, :, 2 * width :] = side


def grads_kernel(got_ref, w_ref, grads_ref, onehot_ref, count_ref, back_ref):
    tokens = got_ref.shape[0]
    width = w_ref.shape[1]
    side = got_ref[:, width:]
    sub = lax.broadcasted_iota(jnp.int32, (tokens, LANES), 0) % 8
    lane = lax.broadcasted_iota(jnp.int32, (tokens, LANES), 1)
    group = (
        lax.broadcasted_iota(jnp.int32, (tokens, 64), 0) // 8 == lax.broadcasted_iota(jnp.int32, (tokens, 64), 1)
    )
    group = group.astype(F32).astype(BF)
    down_rows = (((0,), (0,)), ((), ()))
    wide = jnp.where(sub == width // LANES, side.astype(F32), 0.0).astype(BF)
    routes = lax.dot_general(group, wide, down_rows, preferred_element_type=F32).astype(BF)
    routes = jnp.dot(group, routes, preferred_element_type=F32)
    route = jnp.sum(jnp.where(lane == sub, routes, 0.0), axis=1, keepdims=True).astype(jnp.int32)
    dp_of = (lax.broadcasted_iota(jnp.int32, (tokens, 1), 0) // 8) % 8
    image = ((route % 2) * 4 + route // 2) * 8 + dp_of
    onehot = (image == lax.broadcasted_iota(jnp.int32, (tokens, 64), 1)).astype(F32).astype(BF)
    ones = jnp.ones((tokens, LANES), BF)
    count = jnp.maximum(lax.dot_general(onehot, ones, down_rows, preferred_element_type=F32)[:, :1], 1.0)
    onehot_ref[...] = onehot
    count_ref[...] = count
    for j in range(width // LANES):
        piece = jnp.where(sub == j, side.astype(F32), 0.0).astype(BF)
        pool = lax.dot_general(group, piece, down_rows, preferred_element_type=F32)
        image_grad = (pool / count).astype(BF)
        returned = jnp.dot(onehot, image_grad, preferred_element_type=F32)
        cols = slice(j * LANES, (j + 1) * LANES)
        grads_ref[:, cols] = (got_ref[:, cols].astype(F32) + returned).astype(BF)
    back_ref[...] = lax.dot_general(
        grads_ref[...], w_ref[...], (((1,), (1,)), ((), ())), preferred_element_type=F32
    ).astype(BF)


def down_kernel(core_ref, mix_ref, w_ref, onehot_ref, count_ref, own_ref, sent_ref, back_ref, back_bf_ref):
    hid, width = w_ref.shape
    core = core_ref[0]
    back = mix_ref[0, :, hid:].astype(F32)
    for k in range(1, mix_ref.shape[0]):
        back = back + mix_ref[k, :, hid:].astype(F32)
    back_ref[...] = back
    back_bf_ref[...] = back.astype(BF)
    parts = []
    total = None
    for which in (core, 1 - core):
        rows = mix_ref[pl.ds(2 * which, 2), :, :hid].reshape(256, hid)
        part = jnp.dot(rows, w_ref[...], preferred_element_type=F32).astype(BF)
        marks = onehot_ref[pl.ds(pl.multiple_of(which * 256, 256), 256), :]
        image = lax.dot_general(marks, part, (((0,), (0,)), ((), ())), preferred_element_type=F32)
        total = image if total is None else total + image
        parts.append(part)
    mean = (total / count_ref[...]).astype(BF)
    row = lax.broadcasted_iota(jnp.int32, (256, 64), 0)
    image_of = lax.broadcasted_iota(jnp.int32, (256, 64), 1)
    sub = lax.broadcasted_iota(jnp.int32, (256, LANES), 0) % 8
    for which, part, ref in ((core, parts[0], own_ref), (1 - core, parts[1], sent_ref)):
        pick = ((row // 8 + which * 32) == image_of).astype(F32).astype(BF)
        wide = jnp.dot(pick, mean, preferred_element_type=F32)
        packed = jnp.zeros((256, LANES), F32)
        for j in range(width // LANES):
            packed = jnp.where(sub == j, wide[:, j * LANES : (j + 1) * LANES], packed)
        ref[:, :width] = part
        ref[:, width:] = packed.astype(BF)


def local(patches, w_up, w_down, owner_route, tok_grad, pool_grad):
    tok, width = patches.shape
    hid = w_up.shape[1]
    pieces = width // LANES

    got = pl.pallas_call(
        pack_kernel,
        out_shape=jax.ShapeDtypeStruct((8, tok, 2 * width + LANES), BF),
        in_specs=[pl.BlockSpec(memory_space=pltpu.SMEM)] + [pl.BlockSpec(memory_space=pltpu.VMEM)] * 3,
        cost_estimate=pl.CostEstimate(flops=100_000, bytes_accessed=300_000, transcendentals=0),
    )(owner_route, patches, tok_grad, pool_grad)
    got = exchange(got, "dp")
    got = got.reshape(64, 2 * width + LANES)
    got = gather(got, "row", X_GROUPS)
    rows = gather(got[:, :width], "row", CORE_GROUPS)

    up = jnp.dot(rows, w_up, preferred_element_type=F32) * UP_SCALE
    up = up.astype(F16)
    up = exchange(up.reshape(4, 128, hid), "col", Y_GROUPS)
    up = jnp.sum(up.astype(F32), axis=0).astype(F16)
    other = lax.ppermute(up, "col", Z_SWAP)
    own_g, _ = lax.optimization_barrier((got[:, width:], up))

    got_g = gather(own_g, "row", CORE_GROUPS)
    grads, onehot, count, back = pl.pallas_call(
        grads_kernel,
        out_shape=[
            jax.ShapeDtypeStruct((512, width), BF),
            jax.ShapeDtypeStruct((512, 64), BF),
            jax.ShapeDtypeStruct((64, 1), F32),
            jax.ShapeDtypeStruct((512, hid), BF),
        ],
        in_specs=[pl.BlockSpec(memory_space=pltpu.VMEM)] * 2,
        compiler_params=pltpu.CompilerParams(vmem_limit_bytes=24 * 1024 * 1024),
        cost_estimate=pl.CostEstimate(flops=1_000_000, bytes_accessed=100_000, transcendentals=0),
    )(got_g, w_down)

    v = (up.astype(F32) + other.astype(F32)) * (1.0 / UP_SCALE)
    s = jnp.tanh(GELU_SCALE * (v + 0.044715 * v * v * v))
    hidden = (0.5 * v * (1.0 + s)).astype(BF)
    slope = 0.5 * (1.0 + s) + 0.5 * v * (1.0 - s * s) * GELU_SCALE * (1.0 + 3.0 * 0.044715 * v * v)

    mix = jnp.concatenate(
        [jnp.broadcast_to(hidden[None], (4, 128, hid)), back.reshape(4, 128, hid)], axis=2
    )
    mix = exchange(mix, "col", Y_GROUPS)
    hidden = mix[:, :, :hid].reshape(512, hid)
    core = lax.axis_index("row") % 2
    wide = width + LANES
    own, sent, back, back_bf = pl.pallas_call(
        down_kernel,
        out_shape=[jax.ShapeDtypeStruct((256, wide), BF)] * 2
        + [jax.ShapeDtypeStruct((128, hid), F32), jax.ShapeDtypeStruct((128, hid), BF)],
        in_specs=[pl.BlockSpec(memory_space=pltpu.SMEM)] + [pl.BlockSpec(memory_space=pltpu.VMEM)] * 4,
        compiler_params=pltpu.CompilerParams(vmem_limit_bytes=24 * 1024 * 1024),
        cost_estimate=pl.CostEstimate(flops=400_000_000, bytes_accessed=3_000_000, transcendentals=0),
    )(core.astype(jnp.int32).reshape(1), mix, w_down, onehot, count)
    sent = gather(sent, "row", CORE_GROUPS).reshape(2, 256, wide)
    half = own.astype(F32) + lax.dynamic_index_in_dim(sent, 1 - core, 0, keepdims=False).astype(F32)
    half = half.astype(BF).reshape(4, 64, wide)
    back_bf, _ = lax.optimization_barrier((back_bf, half))
    half = exchange(half, "row", X_GROUPS)
    half = jnp.sum(half.astype(F32), axis=0).astype(BF).reshape(8, tok, width + LANES)

    back_other = lax.ppermute(back_bf, "col", Z_SWAP)
    gp = ((back + back_other.astype(F32)) * slope).astype(BF)
    grad_down = lax.dot_general(hidden, grads, (((0,), (0,)), ((), ())), preferred_element_type=F32)
    half, grad_down = lax.optimization_barrier((half, grad_down))
    last = exchange(half, "dp")
    last = jnp.sum(last.astype(F32), axis=0)
    mixed = last[:, :width].astype(BF)
    pooled = last[:pieces, width:].reshape(1, width)

    y = lax.axis_index("col") % 4
    gps = [gp] + [
        lax.ppermute(gp, "col", [(i, i // 4 * 4 + (i - k) % 4) for i in range(8)]) for k in (1, 2, 3)
    ]
    turned = lax.dynamic_slice(jnp.concatenate([rows, rows], axis=0), (y * 128, 0), (512, width))
    grad_up = lax.dot_general(
        turned, jnp.concatenate(gps, axis=0), (((0,), (0,)), ((), ())), preferred_element_type=F32
    )
    return (mixed, pooled, grad_up, grad_down)


def solution(mesh):
    in_specs = (
        P(("dp", "row"), "col"),
        P("col", ("dp", "row")),
        P(("dp", "row"), "col"),
        P(("dp", "row")),
        P(("dp", "row"), "col"),
        P(("dp", "row"), "col"),
    )
    out_specs = (
        P(("dp", "row"), "col"),
        P(("dp", "row"), "col"),
        P("col", ("dp", "row")),
        P(("dp", "row"), "col"),
    )
    return jax.shard_map(local, mesh=mesh, in_specs=in_specs, out_specs=out_specs, check_vma=False)
```

time: 143 us -> 139 us (0.972)
  the two profiles are of different devices: /device:TPU:66 before, /device:TPU:1 now
where the time goes in v4:
time: 139 us; the launch traced here: 137 us
  blocking collectives  53.9 us (39%)
  starting transfers between devices  40.8 us (29%)
  waiting for transfers between devices  26.3 us (19%)
  matrix products  4.93 us (4%)
  Pallas kernels  4.7 us (3%)
  other arithmetic  2.88 us (2%)
  local copies, waits for them, and re-layouts  2.23 us (2%)
    all_gather x4, blocking collectives, gather(): lax.all_gather(block, axis, axis=0, tiled=True, axis_index_groups=groups)  29.5 us
    all_to_all x1, blocking collectives, exchange(): lax.all_to_all(blocks, axis, split_axis=0, concat_axis=0, tiled=True, axi...  24.4 us
    all_to_all x4, waiting for transfers between devices, exchange(): lax.all_to_all(blocks, axis, split_axis=0, concat_axis=0, tiled=True, axi...  17.5 us
    all_to_all x4, starting transfers between devices, exchange(): lax.all_to_all(blocks, axis, split_axis=0, concat_axis=0, tiled=True, axi...  14.5 us
    ppermute x1, starting transfers between devices, local(): back_other = lax.ppermute(back_bf, 'col', Z_SWAP)  9.98 us
    ppermute x3, starting transfers between devices, local(): lax.ppermute(gp, 'col', [(i, i // 4 * 4 + (i - k) % 4) for i in range(8)])  8.42 us
    ppermute x1, starting transfers between devices, local(): other = lax.ppermute(up, 'col', Z_SWAP)  7.94 us
    ppermute x1, waiting for transfers between devices, local(): other = lax.ppermute(up, 'col', Z_SWAP)  4.34 us
  transfers between devices with their start and end apart: 9, of which 6 were waited for; matrix products, arithmetic and copies ran while one was open for 3% of the time, Pallas kernels for 2%

profile of v4, /device:TPU:1, one launch (start us, length us, event | category | flops | bytes accessed | tf_op | source)
XLA Modules:
  0.0 136.6 jit_solution(4971170313696828440)
XLA Ops:
  0.6 1.5 %shard_map.93 = bf16[8,8,1664]{2,1,0:T(8,128)(2,1)} custom-call(s32[8]{0:T(128)} %route_ref.1, bf16[8,768]{1,0:T(8,128)(2,1)} %patches_ref.1, bf16[8,768]{1,0:T(8,128)(2,1)} %tgrad_ref.1, bf16[1,768]{1,0:T(2,128)(2,1)} %pool_ref.1), custom_call_target="tpu_custom_call" | custom-call | flops 100000 | bytes 300000 | tf_op jit(solution)/shard_map/pallas_call | solution.py:126
  2.1 24.4 %all_to_all.25 = bf16[8,8,1664]{2,1,0:T(8,128)(2,1)S(1)} all-to-all(bf16[8,8,1664]{2,1,0:T(8,128)(2,1)} %shard_map.93), channel_id=1, replica_groups=mesh['dp'=8,'row'=8,'col'=8] {'dp'}, dimensions={0} | all-to-all | bytes 425984 | tf_op jit(solution)/shard_map/all_to_all | solution.py:34
  26.6 11.4 %all_gather.12 = bf16[256,1664]{1,0:T(8,128)(2,1)S(1)} all-gather(bf16[64,1664]{1,0:T(8,128)(2,1)S(1)} %bitcast.25), channel_id=1, replica_groups={{0,16,32,48},{8,24,40,56},{1,17,33,49},{9,25,41,57},{2,18,34,50},{10,26..., dimensions={0}, use_global_device_ids=true | all-gather | bytes 1064960 | tf_op jit(solution)/shard_map/all_gather | solution.py:30
  38.0 9.0 %all_gather.13 = bf16[512,768]{1,0:T(8,128)(2,1)S(1)} all-gather(bf16[256,768]{1,0:T(8,128)(2,1)S(1)} %slice.21), channel_id=1, replica_groups={{0,8},{16,24},{32,40},{48,56},{1,9},{17,25},{33,41},{49,57},{2,10},{18,..., dimensions={0}, use_global_device_ids=true | all-gather | bytes 1179648 | tf_op jit(solution)/shard_map/all_gather | solution.py:30
  47.0 0.9 copy-done.2
  47.9 1.3 fusion
  49.2 4.2 %all-to-all-start.1 = ((f16[4,128,384]{2,1,0:T(8,128)(2,1)}), f16[4,128,384]{2,1,0:T(8,128)(2,1)S(1)}, u32[]{:S(2)}, u32[]{:S(2)}) async-start(f16[4,128,384]{2,1,0:T(8,128)(2,1)} %bitcast.2), calls=%async_computation.1 | async-start | bytes 786432 | tf_op jit(solution)/shard_map/all_to_all | solution.py:34
  53.4 7.2 %all-to-all-done.1 = f16[4,128,384]{2,1,0:T(8,128)(2,1)S(1)} async-done(((f16[4,128,384]{2,1,0:T(8,128)(2,1)}), f16[4,128,384]{2,1,0:T(8,128)(2,1)S(1)}, u32[]{:S(2)}, u32[]{:S(2)}) %all-to-all-start.1) | async-done | bytes 393248 | tf_op jit(solution)/shard_map/all_to_all | solution.py:34
  60.7 7.9 %collective-permute-start = (f16[128,384]{1,0:T(8,128)(2,1)S(1)}, f16[128,384]{1,0:T(8,128)(2,1)S(1)}, u32[]{:S(2)}, u32[]{:S(2)}) collective-permute-start(f16[128,384]{1,0:T(8,128)(2,1)S(1)} %convert_element_type.44), channel_id=1, source_target_pairs={{0,4},{1,5},{2,6},{3,7},{4,0},{5,1},{6,2},{7,3},{8,12},{9,13},{10,... | collective-permute-start | bytes 294920 | tf_op jit(solution)/shard_map/ppermute | solution.py:141
  68.6 4.2 %all_gather.14.got_ref = bf16[512,896]{1,0:T(8,128)(2,1)S(1)} all-gather(bf16[256,896]{1,0:T(8,128)(2,1)S(1)} %slice.22), channel_id=1, replica_groups={{0,8},{16,24},{32,40},{48,56},{1,9},{17,25},{33,41},{49,57},{2,10},{18,..., dimensions={0}, use_global_device_ids=true | all-gather | bytes 1376256 | tf_op jit(solution)/shard_map/all_gather | solution.py:30
  72.8 2.1 %shard_map.94 = (bf16[512,768]{1,0:T(8,128)(2,1)S(1)}, bf16[512,64]{1,0:T(8,128)(2,1)S(1)}, f32[64,1]{1,0:T(8,128)S(1)}, bf16[512,384]{1,0:T(8,128)(2,1)S(1)}) custom-call(bf16[512,896]{1,0:T(8,128)(2,1)S(1)} %all_gather.14.got_ref, bf16[384,768]{1,0:T(8,128)(2,1)S(1)} %copy-done.1), custom_call_target="tpu_custom_call" | custom-call | flops 1000000 | bytes 100000 | tf_op jit(solution)/shard_map/pallas_call | solution.py:145
  74.9 4.3 %collective-permute-done = f16[128,384]{1,0:T(8,128)(2,1)S(1)} collective-permute-done((f16[128,384]{1,0:T(8,128)(2,1)S(1)}, f16[128,384]{1,0:T(8,128)(2,1)S(1)}, u32[]{:S(2)}, u32[]{:S(2)}) %collective-permute-start) | collective-permute-done | bytes 98336 | tf_op jit(solution)/shard_map/ppermute | solution.py:141
  79.3 0.9 pad_maximum_fusion
  80.3 3.5 %all-to-all-start.2 = ((bf16[4,128,768]{2,1,0:T(8,128)(2,1)}), bf16[4,128,768]{2,1,0:T(8,128)(2,1)S(1)}, u32[]{:S(2)}, u32[]{:S(2)}) async-start(bf16[4,128,768]{2,1,0:T(8,128)(2,1)} %pad_maximum_fusion), calls=%async_computation.2 | async-start | bytes 1572864 | tf_op jit(solution)/shard_map/all_to_all | solution.py:34
  83.8 10.4 %all-to-all-done.2.mix_ref = bf16[4,128,768]{2,1,0:T(8,128)(2,1)S(1)} async-done(((bf16[4,128,768]{2,1,0:T(8,128)(2,1)}), bf16[4,128,768]{2,1,0:T(8,128)(2,1)S(1)}, u32[]{:S(2)}, u32[]{:S(2)}) %all-to-all-start.2) | async-done | bytes 786464 | tf_op jit(solution)/shard_map/all_to_all | solution.py:34
  94.2 1.1 shard_map.95
  95.3 4.9 %all_gather.15 = bf16[512,896]{1,0:T(8,128)(2,1)S(1)} all-gather(bf16[256,896]{1,0:T(8,128)(2,1)S(1)} %get-tuple-element.21), channel_id=1, replica_groups={{0,8},{16,24},{32,40},{48,56},{1,9},{17,25},{33,41},{49,57},{2,10},{18,..., dimensions={0}, use_global_device_ids=true | all-gather | bytes 1376256 | tf_op jit(solution)/shard_map/all_gather | solution.py:30
  100.2 0.9 fusion.1
  101.1 3.5 %all-to-all-start.3 = ((bf16[4,64,896]{2,1,0:T(8,128)(2,1)}), bf16[4,64,896]{2,1,0:T(8,128)(2,1)S(1)}, u32[]{:S(2)}, u32[]{:S(2)}) async-start(bf16[4,64,896]{2,1,0:T(8,128)(2,1)} %bitcast.23), calls=%async_computation.3 | async-start | bytes 917504 | tf_op jit(solution)/shard_map/all_to_all | solution.py:34
  104.6 10.0 %collective-permute-start.1 = (bf16[128,384]{1,0:T(8,128)(2,1)S(1)}, bf16[128,384]{1,0:T(8,128)(2,1)S(1)}, u32[]{:S(2)}, u32[]{:S(2)}) collective-permute-start(bf16[128,384]{1,0:T(8,128)(2,1)S(1)} %get-tuple-element.26), channel_id=1, source_target_pairs={{0,4},{1,5},{2,6},{3,7},{4,0},{5,1},{6,2},{7,3},{8,12},{9,13},{10,... | collective-permute-start | bytes 294920 | tf_op jit(solution)/shard_map/ppermute | solution.py:185
  114.6 1.5 %fusion.17 = f32[384,768]{1,0:T(8,128)} fusion(bf16[512,384]{1,0:T(8,128)(2,1)S(1)} %bitcast.24, bf16[512,768]{1,0:T(8,128)(2,1)S(1)} %get-tuple-element.22), kind=kOutput, calls=%fused_computation.30 | convolution fusion | flops 301989888 | bytes 2359296 | tf_op jit(solution)/shard_map/dot_general | solution.py:187
  116.1 0.7 reduce_sum.31
  116.9 3.4 %all-to-all-start.4 = ((bf16[8,8,896]{2,1,0:T(8,128)(2,1)}), bf16[8,8,896]{2,1,0:T(8,128)(2,1)S(1)}, u32[]{:S(2)}, u32[]{:S(2)}) async-start(bf16[8,8,896]{2,1,0:T(8,128)(2,1)} %bitcast.7), calls=%async_computation.4 | async-start | bytes 229376 | tf_op jit(solution)/shard_map/all_to_all | solution.py:34
  120.2 1.5 %collective-permute-done.1 = bf16[128,384]{1,0:T(8,128)(2,1)S(1)} collective-permute-done((bf16[128,384]{1,0:T(8,128)(2,1)S(1)}, bf16[128,384]{1,0:T(8,128)(2,1)S(1)}, u32[]{:S(2)}, u32[]{:S(2)}) %collective-permute-start.1) | collective-permute-done | bytes 98336 | tf_op jit(solution)/shard_map/ppermute | solution.py:185
  121.9 2.2 %collective-permute-start.4 = (bf16[128,384]{1,0:T(8,128)(2,1)S(1)}, bf16[128,384]{1,0:T(8,128)(2,1)S(1)}, u32[]{:S(2)}, u32[]{:S(2)}) collective-permute-start(bf16[128,384]{1,0:T(8,128)(2,1)S(1)} %multiply_convert_fusion), channel_id=1, source_target_pairs={{0,1},{1,2},{2,3},{3,0},{4,5},{5,6},{6,7},{7,4},{8,9},{9,10},{10,1... | collective-permute-start | bytes 294920 | tf_op jit(solution)/shard_map/ppermute | solution.py:196
  124.1 3.7 %collective-permute-start.3 = (bf16[128,384]{1,0:T(8,128)(2,1)S(1)}, bf16[128,384]{1,0:T(8,128)(2,1)S(1)}, u32[]{:S(2)}, u32[]{:S(2)}) collective-permute-start(bf16[128,384]{1,0:T(8,128)(2,1)S(1)} %multiply_convert_fusion), channel_id=1, source_target_pairs={{0,2},{1,3},{2,0},{3,1},{4,6},{5,7},{6,4},{7,5},{8,10},{9,11},{10,... | collective-permute-start | bytes 294920 | tf_op jit(solution)/shard_map/ppermute | solution.py:196
  127.8 2.5 %collective-permute-start.2 = (bf16[128,384]{1,0:T(8,128)(2,1)S(1)}, bf16[128,384]{1,0:T(8,128)(2,1)S(1)}, u32[]{:S(2)}, u32[]{:S(2)}) collective-permute-start(bf16[128,384]{1,0:T(8,128)(2,1)S(1)} %multiply_convert_fusion), channel_id=1, source_target_pairs={{0,3},{1,0},{2,1},{3,2},{4,7},{5,4},{6,5},{7,6},{8,11},{9,8},{10,9... | collective-permute-start | bytes 294920 | tf_op jit(solution)/shard_map/ppermute | solution.py:196
  130.3 0.9 collective-permute-done.3
  131.2 2.1 %collective-permute-done.2 = bf16[128,384]{1,0:T(8,128)(2,1)S(1)} collective-permute-done((bf16[128,384]{1,0:T(8,128)(2,1)S(1)}, bf16[128,384]{1,0:T(8,128)(2,1)S(1)}, u32[]{:S(2)}, u32[]{:S(2)}) %collective-permute-start.2) | collective-permute-done | bytes 98336 | tf_op jit(solution)/shard_map/ppermute | solution.py:196
  133.3 2.1 %fusion.3 = f32[768,384]{1,0:T(8,128)} fusion(s32[]{:T(128)S(6)} %select_n.21, bf16[512,768]{1,0:T(8,128)(2,1)S(1)} %copy-done.3, bf16[128,384]{1,0:T(8,128)(2,1)S(1)} %collective-permute-done.4, bf16[128,384]{1,0:T(8,128)(2,1)S(1)} %collective-permute-done.3, bf16[128,384]{1,0:T(8,128)(2,1)S(1)} %collective-permute-done.2, ...), kind=kOutput, calls=%fused_computation.7 | convolution fusion | flops 305135616 | bytes 2359300 | tf_op jit(solution)/shard_map/dot_general | solution.py:199
  135.4 0.6 slice.28
  136.0 0.6 copy.12
  (20 shorter events, 0.5 us)
Async XLA Ops:
  0.6 47.2 %copy-start = (bf16[768,384]{1,0:T(8,128)(2,1)S(1)}, bf16[768,384]{1,0:T(8,128)(2,1)}, u32[]{:S(2)}) copy-start(bf16[768,384]{1,0:T(8,128)(2,1)} %param.7) | copy-start | bytes 1769476
  47.0 0.9 copy-start.2
  49.2 11.4 %all-to-all-start.1 = ((f16[4,128,384]{2,1,0:T(8,128)(2,1)}), f16[4,128,384]{2,1,0:T(8,128)(2,1)S(1)}, u32[]{:S(2)}, u32[]{:S(2)}) async-start(f16[4,128,384]{2,1,0:T(8,128)(2,1)} %bitcast.2), calls=%async_computation.1 | async-start | bytes 786432 | tf_op jit(solution)/shard_map/all_to_all | solution.py:34
  53.4 19.4 %copy-start.1 = (bf16[384,768]{1,0:T(8,128)(2,1)S(1)}, bf16[384,768]{1,0:T(8,128)(2,1)}, u32[]{:S(2)}) copy-start(bf16[384,768]{1,0:T(8,128)(2,1)} %w_ref.3) | copy-start | bytes 1769476
  60.7 18.5 %collective-permute-start = (f16[128,384]{1,0:T(8,128)(2,1)S(1)}, f16[128,384]{1,0:T(8,128)(2,1)S(1)}, u32[]{:S(2)}, u32[]{:S(2)}) collective-permute-start(f16[128,384]{1,0:T(8,128)(2,1)S(1)} %convert_element_type.44), channel_id=1, source_target_pairs={{0,4},{1,5},{2,6},{3,7},{4,0},{5,1},{6,2},{7,3},{8,12},{9,13},{10,... | collective-permute-start | bytes 294920 | tf_op jit(solution)/shard_map/ppermute | solution.py:141
  80.3 13.9 %all-to-all-start.2 = ((bf16[4,128,768]{2,1,0:T(8,128)(2,1)}), bf16[4,128,768]{2,1,0:T(8,128)(2,1)S(1)}, u32[]{:S(2)}, u32[]{:S(2)}) async-start(bf16[4,128,768]{2,1,0:T(8,128)(2,1)} %pad_maximum_fusion), calls=%async_computation.2 | async-start | bytes 1572864 | tf_op jit(solution)/shard_map/all_to_all | solution.py:34
  101.1 15.0 %all-to-all-start.3 = ((bf16[4,64,896]{2,1,0:T(8,128)(2,1)}), bf16[4,64,896]{2,1,0:T(8,128)(2,1)S(1)}, u32[]{:S(2)}, u32[]{:S(2)}) async-start(bf16[4,64,896]{2,1,0:T(8,128)(2,1)} %bitcast.23), calls=%async_computation.3 | async-start | bytes 917504 | tf_op jit(solution)/shard_map/all_to_all | solution.py:34
  104.6 17.1 %collective-permute-start.1 = (bf16[128,384]{1,0:T(8,128)(2,1)S(1)}, bf16[128,384]{1,0:T(8,128)(2,1)S(1)}, u32[]{:S(2)}, u32[]{:S(2)}) collective-permute-start(bf16[128,384]{1,0:T(8,128)(2,1)S(1)} %get-tuple-element.26), channel_id=1, source_target_pairs={{0,4},{1,5},{2,6},{3,7},{4,0},{5,1},{6,2},{7,3},{8,12},{9,13},{10,... | collective-permute-start | bytes 294920 | tf_op jit(solution)/shard_map/ppermute | solution.py:185
  116.1 17.2 %copy-start.3 = (bf16[512,768]{1,0:T(8,128)(2,1)S(1)}, bf16[512,768]{1,0:T(8,128)(2,1)}, u32[]{:S(2)}) copy-start(bf16[512,768]{1,0:T(8,128)(2,1)} %copy-done.2) | copy-start | bytes 2359300
  116.9 18.5 %all-to-all-start.4 = ((bf16[8,8,896]{2,1,0:T(8,128)(2,1)}), bf16[8,8,896]{2,1,0:T(8,128)(2,1)S(1)}, u32[]{:S(2)}, u32[]{:S(2)}) async-start(bf16[8,8,896]{2,1,0:T(8,128)(2,1)} %bitcast.7), calls=%async_computation.4 | async-start | bytes 229376 | tf_op jit(solution)/shard_map/all_to_all | solution.py:34
  121.9 8.5 %collective-permute-start.4 = (bf16[128,384]{1,0:T(8,128)(2,1)S(1)}, bf16[128,384]{1,0:T(8,128)(2,1)S(1)}, u32[]{:S(2)}, u32[]{:S(2)}) collective-permute-start(bf16[128,384]{1,0:T(8,128)(2,1)S(1)} %multiply_convert_fusion), channel_id=1, source_target_pairs={{0,1},{1,2},{2,3},{3,0},{4,5},{5,6},{6,7},{7,4},{8,9},{9,10},{10,1... | collective-permute-start | bytes 294920 | tf_op jit(solution)/shard_map/ppermute | solution.py:196
  124.1 7.2 %collective-permute-start.3 = (bf16[128,384]{1,0:T(8,128)(2,1)S(1)}, bf16[128,384]{1,0:T(8,128)(2,1)S(1)}, u32[]{:S(2)}, u32[]{:S(2)}) collective-permute-start(bf16[128,384]{1,0:T(8,128)(2,1)S(1)} %multiply_convert_fusion), channel_id=1, source_target_pairs={{0,2},{1,3},{2,0},{3,1},{4,6},{5,7},{6,4},{7,5},{8,10},{9,11},{10,... | collective-permute-start | bytes 294920 | tf_op jit(solution)/shard_map/ppermute | solution.py:196
  127.8 5.5 %collective-permute-start.2 = (bf16[128,384]{1,0:T(8,128)(2,1)S(1)}, bf16[128,384]{1,0:T(8,128)(2,1)S(1)}, u32[]{:S(2)}, u32[]{:S(2)}) collective-permute-start(bf16[128,384]{1,0:T(8,128)(2,1)S(1)} %multiply_convert_fusion), channel_id=1, source_target_pairs={{0,3},{1,0},{2,1},{3,2},{4,7},{5,4},{6,5},{7,6},{8,11},{9,8},{10,9... | collective-permute-start | bytes 294920 | tf_op jit(solution)/shard_map/ppermute | solution.py:196

commit v5 on v4

--- a/solution.py
+++ b/solution.py
@@ -53,8 +53,11 @@
         out_ref[k, :, 2 * width :] = side
 
 
-def grads_kernel(got_ref, w_ref, grads_ref, onehot_ref, count_ref, back_ref):
+def grads_kernel(y_ref, rows_ref, got_ref, w_ref, turned_ref, grads_ref, onehot_ref, count_ref, back_ref):
     tokens = got_ref.shape[0]
+    for k in range(4):
+        start = pl.multiple_of(((y_ref[0] + k) % 4) * 128, 128)
+        turned_ref[k * 128 : (k + 1) * 128, :] = rows_ref[pl.ds(start, 128), :]
     width = w_ref.shape[1]
     side = got_ref[:, width:]
     sub = lax.broadcasted_iota(jnp.int32, (tokens, LANES), 0) % 8
@@ -142,18 +145,20 @@
     own_g, _ = lax.optimization_barrier((got[:, width:], up))
 
     got_g = gather(own_g, "row", CORE_GROUPS)
-    grads, onehot, count, back = pl.pallas_call(
+    y = lax.axis_index("col") % 4
+    turned, grads, onehot, count, back = pl.pallas_call(
         grads_kernel,
         out_shape=[
+            jax.ShapeDtypeStruct((512, width), BF),
             jax.ShapeDtypeStruct((512, width), BF),
             jax.ShapeDtypeStruct((512, 64), BF),
             jax.ShapeDtypeStruct((64, 1), F32),
             jax.ShapeDtypeStruct((512, hid), BF),
         ],
-        in_specs=[pl.BlockSpec(memory_space=pltpu.VMEM)] * 2,
+        in_specs=[pl.BlockSpec(memory_space=pltpu.SMEM)] + [pl.BlockSpec(memory_space=pltpu.VMEM)] * 3,
         compiler_params=pltpu.CompilerParams(vmem_limit_bytes=24 * 1024 * 1024),
         cost_estimate=pl.CostEstimate(flops=1_000_000, bytes_accessed=100_000, transcendentals=0),
-    )(got_g, w_down)
+    )(y.astype(jnp.int32).reshape(1), rows, got_g, w_down)
 
     v = (up.astype(F32) + other.astype(F32)) * (1.0 / UP_SCALE)
     s = jnp.tanh(GELU_SCALE * (v + 0.044715 * v * v * v))
@@ -191,11 +196,9 @@
     mixed = last[:, :width].astype(BF)
     pooled = last[:pieces, width:].reshape(1, width)
 
-    y = lax.axis_index("col") % 4
     gps = [gp] + [
         lax.ppermute(gp, "col", [(i, i // 4 * 4 + (i - k) % 4) for i in range(8)]) for k in (1, 2, 3)
     ]
-    turned = lax.dynamic_slice(jnp.concatenate([rows, rows], axis=0), (y * 128, 0), (512, width))
     grad_up = lax.dot_general(
         turned, jnp.concatenate(gps, axis=0), (((0,), (0,)), ((), ())), preferred_element_type=F32
     )

time: 139 us -> 139 us (level)
  the two profiles are of different devices: /device:TPU:1 before, /device:TPU:66 now
where the time goes in v5:
time: 139 us; the launch traced here: 138 us
  starting transfers between devices  47.4 us (34%)
  blocking collectives  46 us (33%)
  waiting for transfers between devices  28.9 us (21%)
  Pallas kernels  4.73 us (3%)
  matrix products  4.45 us (3%)
  other arithmetic  3.9 us (3%)
  local copies, waits for them, and re-layouts  2.22 us (2%)
    all_to_all x1, blocking collectives, exchange(): lax.all_to_all(blocks, axis, split_axis=0, concat_axis=0, tiled=True, axi...  25.2 us
    all_to_all x4, starting transfers between devices, exchange(): lax.all_to_all(blocks, axis, split_axis=0, concat_axis=0, tiled=True, axi...  22.9 us
    all_gather x4, blocking collectives, gather(): lax.all_gather(block, axis, axis=0, tiled=True, axis_index_groups=groups)  20.8 us
    all_to_all x4, waiting for transfers between devices, exchange(): lax.all_to_all(blocks, axis, split_axis=0, concat_axis=0, tiled=True, axi...  17.9 us
    ppermute x3, starting transfers between devices, local(): lax.ppermute(gp, 'col', [(i, i // 4 * 4 + (i - k) % 4) for i in range(8)])  8.98 us
    ppermute x1, starting transfers between devices, local(): other = lax.ppermute(up, 'col', Z_SWAP)  8.22 us
    ppermute x1, starting transfers between devices, local(): back_other = lax.ppermute(back_bf, 'col', Z_SWAP)  7.35 us
    ppermute x1, waiting for transfers between devices, local(): other = lax.ppermute(up, 'col', Z_SWAP)  4.74 us
  transfers between devices with their start and end apart: 9, of which 6 were waited for; matrix products, arithmetic and copies ran while one was open for 3% of the time, Pallas kernels for 2%

profile of v5, /device:TPU:66, one launch (start us, length us, event | category | flops | bytes accessed | tf_op | source)
XLA Modules:
  0.0 138.5 jit_solution(14900263472239442807)
XLA Ops:
  0.6 1.5 %shard_map.93 = bf16[8,8,1664]{2,1,0:T(8,128)(2,1)} custom-call(s32[8]{0:T(128)} %route_ref.1, bf16[8,768]{1,0:T(8,128)(2,1)} %patches_ref.1, bf16[8,768]{1,0:T(8,128)(2,1)} %tgrad_ref.1, bf16[1,768]{1,0:T(2,128)(2,1)} %pool_ref.1), custom_call_target="tpu_custom_call" | custom-call | flops 100000 | bytes 300000 | tf_op jit(solution)/shard_map/pallas_call | solution.py:129
  2.1 25.2 %all_to_all.25 = bf16[8,8,1664]{2,1,0:T(8,128)(2,1)S(1)} all-to-all(bf16[8,8,1664]{2,1,0:T(8,128)(2,1)} %shard_map.93), channel_id=1, replica_groups=mesh['dp'=8,'row'=8,'col'=8] {'dp'}, dimensions={0} | all-to-all | bytes 425984 | tf_op jit(solution)/shard_map/all_to_all | solution.py:34
  27.4 13.5 %all_gather.12 = bf16[256,1664]{1,0:T(8,128)(2,1)S(1)} all-gather(bf16[64,1664]{1,0:T(8,128)(2,1)S(1)} %bitcast.27), channel_id=1, replica_groups={{0,16,32,48},{8,24,40,56},{1,17,33,49},{9,25,41,57},{2,18,34,50},{10,26..., dimensions={0}, use_global_device_ids=true | all-gather | bytes 1064960 | tf_op jit(solution)/shard_map/all_gather | solution.py:30
  40.9 2.4 %all_gather.13.rows_ref = bf16[512,768]{1,0:T(8,128)(2,1)S(1)} all-gather(bf16[256,768]{1,0:T(8,128)(2,1)S(1)} %slice.21), channel_id=1, replica_groups={{0,8},{16,24},{32,40},{48,56},{1,9},{17,25},{33,41},{49,57},{2,10},{18,..., dimensions={0}, use_global_device_ids=true | all-gather | bytes 1179648 | tf_op jit(solution)/shard_map/all_gather | solution.py:30
  43.3 1.3 fusion
  44.6 4.5 %all-to-all-start.1 = ((f16[4,128,384]{2,1,0:T(8,128)(2,1)}), f16[4,128,384]{2,1,0:T(8,128)(2,1)}, u32[]{:S(2)}, u32[]{:S(2)}) async-start(f16[4,128,384]{2,1,0:T(8,128)(2,1)} %bitcast.2), calls=%async_computation.1 | async-start | bytes 786432 | tf_op jit(solution)/shard_map/all_to_all | solution.py:34
  49.1 8.4 %all-to-all-done.1 = f16[4,128,384]{2,1,0:T(8,128)(2,1)} async-done(((f16[4,128,384]{2,1,0:T(8,128)(2,1)}), f16[4,128,384]{2,1,0:T(8,128)(2,1)}, u32[]{:S(2)}, u32[]{:S(2)}) %all-to-all-start.1) | async-done | bytes 393248 | tf_op jit(solution)/shard_map/all_to_all | solution.py:34
  57.6 1.1 convert_reduce_fusion
  58.6 8.2 %collective-permute-start = (f16[128,384]{1,0:T(8,128)(2,1)S(1)}, f16[128,384]{1,0:T(8,128)(2,1)S(1)}, u32[]{:S(2)}, u32[]{:S(2)}) collective-permute-start(f16[128,384]{1,0:T(8,128)(2,1)S(1)} %convert_element_type.44), channel_id=1, source_target_pairs={{0,4},{1,5},{2,6},{3,7},{4,0},{5,1},{6,2},{7,3},{8,12},{9,13},{10,... | collective-permute-start | bytes 294920 | tf_op jit(solution)/shard_map/ppermute | solution.py:144
  66.9 2.5 %all_gather.14.got_ref = bf16[512,896]{1,0:T(8,128)(2,1)S(1)} all-gather(bf16[256,896]{1,0:T(8,128)(2,1)S(1)} %slice.22), channel_id=1, replica_groups={{0,8},{16,24},{32,40},{48,56},{1,9},{17,25},{33,41},{49,57},{2,10},{18,..., dimensions={0}, use_global_device_ids=true | all-gather | bytes 1376256 | tf_op jit(solution)/shard_map/all_gather | solution.py:30
  69.3 2.1 %shard_map.94 = (bf16[512,768]{1,0:T(8,128)(2,1)S(1)}, bf16[512,768]{1,0:T(8,128)(2,1)S(1)}, bf16[512,64]{1,0:T(8,128)(2,1)S(1)}, f32[64,1]{1,0:T(8,128)S(1)}, bf16[512,384]{1,0:T(8,128)(2,1)S(1)}) custom-call(s32[1]{0:T(128)} %bitcast.3.y_ref, bf16[512,768]{1,0:T(8,128)(2,1)S(1)} %all_gather.13.rows_ref, bf16[512,896]{1,0:T(8,128)(2,1)S(1)} %all_gather.14.got_ref, ...), custom_call_target="tpu_custom_call" | custom-call | flops 1000000 | bytes 100000 | tf_op jit(solution)/shard_map/pallas_call | solution.py:149
  71.5 0.9 copy-done.2
  72.3 4.7 %collective-permute-done = f16[128,384]{1,0:T(8,128)(2,1)S(1)} collective-permute-done((f16[128,384]{1,0:T(8,128)(2,1)S(1)}, f16[128,384]{1,0:T(8,128)(2,1)S(1)}, u32[]{:S(2)}, u32[]{:S(2)}) %collective-permute-start) | collective-permute-done | bytes 98336 | tf_op jit(solution)/shard_map/ppermute | solution.py:144
  77.2 0.9 pad_maximum_fusion
  78.1 3.5 %all-to-all-start.2 = ((bf16[4,128,768]{2,1,0:T(8,128)(2,1)}), bf16[4,128,768]{2,1,0:T(8,128)(2,1)S(1)}, u32[]{:S(2)}, u32[]{:S(2)}) async-start(bf16[4,128,768]{2,1,0:T(8,128)(2,1)} %pad_maximum_fusion), calls=%async_computation.2 | async-start | bytes 1572864 | tf_op jit(solution)/shard_map/all_to_all | solution.py:34
  81.7 9.4 %all-to-all-done.2.mix_ref = bf16[4,128,768]{2,1,0:T(8,128)(2,1)S(1)} async-done(((bf16[4,128,768]{2,1,0:T(8,128)(2,1)}), bf16[4,128,768]{2,1,0:T(8,128)(2,1)S(1)}, u32[]{:S(2)}, u32[]{:S(2)}) %all-to-all-start.2) | async-done | bytes 786464 | tf_op jit(solution)/shard_map/all_to_all | solution.py:34
  91.1 1.1 shard_map.95
  92.2 2.5 %all_gather.15 = bf16[512,896]{1,0:T(8,128)(2,1)S(1)} all-gather(bf16[256,896]{1,0:T(8,128)(2,1)S(1)} %get-tuple-element.22), channel_id=1, replica_groups={{0,8},{16,24},{32,40},{48,56},{1,9},{17,25},{33,41},{49,57},{2,10},{18,..., dimensions={0}, use_global_device_ids=true | all-gather | bytes 1376256 | tf_op jit(solution)/shard_map/all_gather | solution.py:30
  94.7 0.9 fusion.1
  95.6 10.3 %all-to-all-start.3 = ((bf16[4,64,896]{2,1,0:T(8,128)(2,1)}), bf16[4,64,896]{2,1,0:T(8,128)(2,1)S(1)}, u32[]{:S(2)}, u32[]{:S(2)}) async-start(bf16[4,64,896]{2,1,0:T(8,128)(2,1)} %bitcast.25), calls=%async_computation.3 | async-start | bytes 917504 | tf_op jit(solution)/shard_map/all_to_all | solution.py:34
  105.9 7.4 %collective-permute-start.1 = (bf16[128,384]{1,0:T(8,128)(2,1)S(1)}, bf16[128,384]{1,0:T(8,128)(2,1)S(1)}, u32[]{:S(2)}, u32[]{:S(2)}) collective-permute-start(bf16[128,384]{1,0:T(8,128)(2,1)S(1)} %get-tuple-element.28), channel_id=1, source_target_pairs={{0,4},{1,5},{2,6},{3,7},{4,0},{5,1},{6,2},{7,3},{8,12},{9,13},{10,... | collective-permute-start | bytes 294920 | tf_op jit(solution)/shard_map/ppermute | solution.py:190
  113.3 1.5 %fusion.14 = f32[384,768]{1,0:T(8,128)} fusion(bf16[512,384]{1,0:T(8,128)(2,1)S(1)} %bitcast.26, bf16[512,768]{1,0:T(8,128)(2,1)S(1)} %get-tuple-element.23), kind=kOutput, calls=%fused_computation.26 | convolution fusion | flops 301989888 | bytes 2359296 | tf_op jit(solution)/shard_map/dot_general | solution.py:192
  114.8 0.7 reduce_sum.31
  115.6 4.6 %all-to-all-start.4 = ((bf16[8,8,896]{2,1,0:T(8,128)(2,1)}), bf16[8,8,896]{2,1,0:T(8,128)(2,1)S(1)}, u32[]{:S(2)}, u32[]{:S(2)}) async-start(bf16[8,8,896]{2,1,0:T(8,128)(2,1)} %bitcast.8), calls=%async_computation.4 | async-start | bytes 229376 | tf_op jit(solution)/shard_map/all_to_all | solution.py:34
  120.2 2.3 %collective-permute-done.1 = bf16[128,384]{1,0:T(8,128)(2,1)S(1)} collective-permute-done((bf16[128,384]{1,0:T(8,128)(2,1)S(1)}, bf16[128,384]{1,0:T(8,128)(2,1)S(1)}, u32[]{:S(2)}, u32[]{:S(2)}) %collective-permute-start.1) | collective-permute-done | bytes 98336 | tf_op jit(solution)/shard_map/ppermute | solution.py:190
  122.7 2.5 %collective-permute-start.4 = (bf16[128,384]{1,0:T(8,128)(2,1)S(1)}, bf16[128,384]{1,0:T(8,128)(2,1)S(1)}, u32[]{:S(2)}, u32[]{:S(2)}) collective-permute-start(bf16[128,384]{1,0:T(8,128)(2,1)S(1)} %multiply_convert_fusion), channel_id=1, source_target_pairs={{0,1},{1,2},{2,3},{3,0},{4,5},{5,6},{6,7},{7,4},{8,9},{9,10},{10,1... | collective-permute-start | bytes 294920 | tf_op jit(solution)/shard_map/ppermute | solution.py:200
  125.2 4.0 %collective-permute-start.3 = (bf16[128,384]{1,0:T(8,128)(2,1)S(1)}, bf16[128,384]{1,0:T(8,128)(2,1)S(1)}, u32[]{:S(2)}, u32[]{:S(2)}) collective-permute-start(bf16[128,384]{1,0:T(8,128)(2,1)S(1)} %multiply_convert_fusion), channel_id=1, source_target_pairs={{0,2},{1,3},{2,0},{3,1},{4,6},{5,7},{6,4},{7,5},{8,10},{9,11},{10,... | collective-permute-start | bytes 294920 | tf_op jit(solution)/shard_map/ppermute | solution.py:200
  129.1 2.5 %collective-permute-start.2 = (bf16[128,384]{1,0:T(8,128)(2,1)S(1)}, bf16[128,384]{1,0:T(8,128)(2,1)S(1)}, u32[]{:S(2)}, u32[]{:S(2)}) collective-permute-start(bf16[128,384]{1,0:T(8,128)(2,1)S(1)} %multiply_convert_fusion), channel_id=1, source_target_pairs={{0,3},{1,0},{2,1},{3,2},{4,7},{5,4},{6,5},{7,6},{8,11},{9,8},{10,9... | collective-permute-start | bytes 294920 | tf_op jit(solution)/shard_map/ppermute | solution.py:200
  131.7 1.5 %collective-permute-done.3 = bf16[128,384]{1,0:T(8,128)(2,1)S(1)} collective-permute-done((bf16[128,384]{1,0:T(8,128)(2,1)S(1)}, bf16[128,384]{1,0:T(8,128)(2,1)S(1)}, u32[]{:S(2)}, u32[]{:S(2)}) %collective-permute-start.3) | collective-permute-done | bytes 98336 | tf_op jit(solution)/shard_map/ppermute | solution.py:200
  133.2 2.5 %collective-permute-done.2 = bf16[128,384]{1,0:T(8,128)(2,1)S(1)} collective-permute-done((bf16[128,384]{1,0:T(8,128)(2,1)S(1)}, bf16[128,384]{1,0:T(8,128)(2,1)S(1)}, u32[]{:S(2)}, u32[]{:S(2)}) %collective-permute-start.2) | collective-permute-done | bytes 98336 | tf_op jit(solution)/shard_map/ppermute | solution.py:200
  135.7 1.6 %fusion.2 = f32[768,384]{1,0:T(8,128)} fusion(bf16[512,768]{1,0:T(8,128)(2,1)S(1)} %copy-done.3, bf16[128,384]{1,0:T(8,128)(2,1)S(1)} %collective-permute-done.4, bf16[128,384]{1,0:T(8,128)(2,1)S(1)} %collective-permute-done.3, bf16[128,384]{1,0:T(8,128)(2,1)S(1)} %collective-permute-done.2, bf16[128,384]{1,0:T(8,128)(2,1)S(1)} %multiply_convert_fusion), kind=kOutput, calls=%fused_computation.6 | convolution fusion | flops 303562752 | bytes 2359296 | tf_op jit(solution)/shard_map/dot_general | solution.py:202
  137.3 0.6 slice.28
  (20 shorter events, 1.1 us)
Async XLA Ops:
  0.6 42.7 %copy-start = (bf16[768,384]{1,0:T(8,128)(2,1)S(1)}, bf16[768,384]{1,0:T(8,128)(2,1)}, u32[]{:S(2)}) copy-start(bf16[768,384]{1,0:T(8,128)(2,1)} %param.7) | copy-start | bytes 1769476
  44.6 12.9 %all-to-all-start.1 = ((f16[4,128,384]{2,1,0:T(8,128)(2,1)}), f16[4,128,384]{2,1,0:T(8,128)(2,1)}, u32[]{:S(2)}, u32[]{:S(2)}) async-start(f16[4,128,384]{2,1,0:T(8,128)(2,1)} %bitcast.2), calls=%async_computation.1 | async-start | bytes 786432 | tf_op jit(solution)/shard_map/all_to_all | solution.py:34
  49.1 20.2 %copy-start.1 = (bf16[384,768]{1,0:T(8,128)(2,1)S(1)}, bf16[384,768]{1,0:T(8,128)(2,1)}, u32[]{:S(2)}) copy-start(bf16[384,768]{1,0:T(8,128)(2,1)} %w_ref.3) | copy-start | bytes 1769476
  58.6 18.4 %collective-permute-start = (f16[128,384]{1,0:T(8,128)(2,1)S(1)}, f16[128,384]{1,0:T(8,128)(2,1)S(1)}, u32[]{:S(2)}, u32[]{:S(2)}) collective-permute-start(f16[128,384]{1,0:T(8,128)(2,1)S(1)} %convert_element_type.44), channel_id=1, source_target_pairs={{0,4},{1,5},{2,6},{3,7},{4,0},{5,1},{6,2},{7,3},{8,12},{9,13},{10,... | collective-permute-start | bytes 294920 | tf_op jit(solution)/shard_map/ppermute | solution.py:144
  71.4 0.9 copy-start.2
  78.1 13.0 %all-to-all-start.2 = ((bf16[4,128,768]{2,1,0:T(8,128)(2,1)}), bf16[4,128,768]{2,1,0:T(8,128)(2,1)S(1)}, u32[]{:S(2)}, u32[]{:S(2)}) async-start(bf16[4,128,768]{2,1,0:T(8,128)(2,1)} %pad_maximum_fusion), calls=%async_computation.2 | async-start | bytes 1572864 | tf_op jit(solution)/shard_map/all_to_all | solution.py:34
  95.6 19.3 %all-to-all-start.3 = ((bf16[4,64,896]{2,1,0:T(8,128)(2,1)}), bf16[4,64,896]{2,1,0:T(8,128)(2,1)S(1)}, u32[]{:S(2)}, u32[]{:S(2)}) async-start(bf16[4,64,896]{2,1,0:T(8,128)(2,1)} %bitcast.25), calls=%async_computation.3 | async-start | bytes 917504 | tf_op jit(solution)/shard_map/all_to_all | solution.py:34
  105.9 16.6 %collective-permute-start.1 = (bf16[128,384]{1,0:T(8,128)(2,1)S(1)}, bf16[128,384]{1,0:T(8,128)(2,1)S(1)}, u32[]{:S(2)}, u32[]{:S(2)}) collective-permute-start(bf16[128,384]{1,0:T(8,128)(2,1)S(1)} %get-tuple-element.28), channel_id=1, source_target_pairs={{0,4},{1,5},{2,6},{3,7},{4,0},{5,1},{6,2},{7,3},{8,12},{9,13},{10,... | collective-permute-start | bytes 294920 | tf_op jit(solution)/shard_map/ppermute | solution.py:190
  114.8 20.8 %copy-start.3 = (bf16[512,768]{1,0:T(8,128)(2,1)S(1)}, bf16[512,768]{1,0:T(8,128)(2,1)}, u32[]{:S(2)}) copy-start(bf16[512,768]{1,0:T(8,128)(2,1)} %copy-done.2) | copy-start | bytes 2359300
  115.6 21.7 %all-to-all-start.4 = ((bf16[8,8,896]{2,1,0:T(8,128)(2,1)}), bf16[8,8,896]{2,1,0:T(8,128)(2,1)S(1)}, u32[]{:S(2)}, u32[]{:S(2)}) async-start(bf16[8,8,896]{2,1,0:T(8,128)(2,1)} %bitcast.8), calls=%async_computation.4 | async-start | bytes 229376 | tf_op jit(solution)/shard_map/all_to_all | solution.py:34
  122.7 9.0 %collective-permute-start.4 = (bf16[128,384]{1,0:T(8,128)(2,1)S(1)}, bf16[128,384]{1,0:T(8,128)(2,1)S(1)}, u32[]{:S(2)}, u32[]{:S(2)}) collective-permute-start(bf16[128,384]{1,0:T(8,128)(2,1)S(1)} %multiply_convert_fusion), channel_id=1, source_target_pairs={{0,1},{1,2},{2,3},{3,0},{4,5},{5,6},{6,7},{7,4},{8,9},{9,10},{10,1... | collective-permute-start | bytes 294920 | tf_op jit(solution)/shard_map/ppermute | solution.py:200
  125.2 8.0 %collective-permute-start.3 = (bf16[128,384]{1,0:T(8,128)(2,1)S(1)}, bf16[128,384]{1,0:T(8,128)(2,1)S(1)}, u32[]{:S(2)}, u32[]{:S(2)}) collective-permute-start(bf16[128,384]{1,0:T(8,128)(2,1)S(1)} %multiply_convert_fusion), channel_id=1, source_target_pairs={{0,2},{1,3},{2,0},{3,1},{4,6},{5,7},{6,4},{7,5},{8,10},{9,11},{10,... | collective-permute-start | bytes 294920 | tf_op jit(solution)/shard_map/ppermute | solution.py:200
  129.1 6.5 %collective-permute-start.2 = (bf16[128,384]{1,0:T(8,128)(2,1)S(1)}, bf16[128,384]{1,0:T(8,128)(2,1)S(1)}, u32[]{:S(2)}, u32[]{:S(2)}) collective-permute-start(bf16[128,384]{1,0:T(8,128)(2,1)S(1)} %multiply_convert_fusion), channel_id=1, source_target_pairs={{0,3},{1,0},{2,1},{3,2},{4,7},{5,4},{6,5},{7,6},{8,11},{9,8},{10,9... | collective-permute-start | bytes 294920 | tf_op jit(solution)/shard_map/ppermute | solution.py:200
